TPU v7x, 512 devices: a whole 4x8x8 slice. The times are simulated.
512 devices in a mesh: slab: 8 (over z), curve: 64 (over y, x, core).
Axes of the slice: x: 4, y: 8, z: 8, core: 2. Of those that a mesh axis runs over, the one named last changes fastest.
Arguments:
- state: float32 [8192, 8, 512], P(('slab', 'curve')), may hold values from -6 to 6
- velocity: bfloat16 [3, 64, 8192], P(None, None, ('slab', 'curve')), may hold values from -4 to 4
- pre_exp: float32 [8192], P(('slab', 'curve')), may hold values from 0.5 to 5
- stoich: float32 [8], replicated, may hold values from -3 to 3
- neighbours: int32 [8192, 6], P(('slab', 'curve')), may hold values from 0 to 8191, as said below
- switch: int32 [8192], P(('slab', 'curve')), may hold values from 0 to 1
- new_owner: int32 [8192], P(('slab', 'curve')), may hold values from 0 to 63, as said below
Outputs:
- state7_out: float32 [6144, 8, 512], P(('slab', 'curve'))
- state3_out: float32 [8192, 512], P(('slab', 'curve'))
Inputs may be any that keep to these rules, and one draw needn't show every extreme that they name: Element g lives on device g // 16 of the mesh flattened slab first. The neighbour across face 0 (1) is on the same device or on the previous (next) curve index with wrap, same slab; across faces 2 and 3 on the same device; across face 4 (5) on the same device or the previous (next) slab with wrap, same curve index. The relation is symmetric: the neighbour of neighbours[g, s] across face s xor 1 is g, and face nodes match in the stated order. Each device has exactly 8 faces 0, 8 faces 1, 16 faces 4 and 16 faces 5 whose neighbour lies on another device. `new_owner`: the new owner is in the same slab: the element's own curve index or one next to it with wrap; elements with switch 1 keep their own. From one device at most 2 elements go to each of its two neighbours, and afterwards a device holds at most 12 elements with switch 0; both bounds are reached in every draw.
All inputs are finite; a program needn't handle non-finite values.
Results may differ from a plain program's by a relative error of at most 0.0005.
Values may be sent and summed in bfloat16 or wider, within the bound.
A program may use at most 64 MiB of HBM per device.

v0:
```python
import functools

import jax
import jax.numpy as jnp
import ml_dtypes
import numpy as np
from jax import lax
from jax.experimental import pallas as pl
from jax.experimental.pallas import tpu as pltpu
from jax.sharding import PartitionSpec as P

P7 = 8
P3 = 4
ELEMS = 16
FIELDS = 8
LANES = ELEMS * FIELDS
HOLD7 = 12
STEP = 0.002
ACTIVATION = 1.5
MESH = pl.DeviceIdType.MESH
F32 = jnp.float32
BF16 = jnp.bfloat16


def lobatto_points(number):
    return -np.cos(np.pi * np.arange(number) / (number - 1))


def derivative_matrix(points):
    number = points.shape[0]
    weights = np.ones(number)
    for row in range(number):
        for col in range(number):
            if col != row:
                weights[row] = weights[row] / (points[row] - points[col])
    matrix = np.zeros((number, number))
    for row in range(number):
        for col in range(number):
            if col != row:
                matrix[row, col] = weights[col] / weights[row] / (points[row] - points[col])
        matrix[row, row] = -np.sum(matrix[row])
    return matrix


def interpolation_matrix(source, target):
    matrix = np.ones((target.shape[0], source.shape[0]))
    for col in range(source.shape[0]):
        for other in range(source.shape[0]):
            if other != col:
                matrix[:, col] = (
                    matrix[:, col] * (target - source[other]) / (source[col] - source[other])
                )
    return matrix


def kron3(a, b, c):
    return np.kron(a, np.kron(b, c))


def to_bf16(matrix):
    return np.asarray(matrix, np.float32).astype(ml_dtypes.bfloat16)


def split_columns(matrix):
    full = np.asarray(matrix, np.float32)
    high = full.astype(ml_dtypes.bfloat16)
    low = (full - high.astype(np.float32)).astype(ml_dtypes.bfloat16)
    return np.concatenate([high, low, high], axis=1)


def face_selectors(extent):
    ident = np.eye(extent)
    first, last = ident[:1], ident[-1:]
    picks = []
    for end in (first, last):
        picks.append(kron3(end, ident, ident))
    for end in (first, last):
        picks.append(kron3(ident, end, ident))
    for end in (first, last):
        picks.append(kron3(ident, ident, end))
    return np.stack(picks)


def make_tables():
    r7, r3 = lobatto_points(P7), lobatto_points(P3)
    d7, d3 = derivative_matrix(r7), derivative_matrix(r3)
    down = interpolation_matrix(r7, r3)
    up = interpolation_matrix(r3, r7)
    i7, i3 = np.eye(P7), np.eye(P3)
    div_i = np.kron(d7, np.eye(32))
    two = np.eye(2)
    div_jk = np.concatenate([np.kron(two, np.kron(d7, i7)), np.kron(two, np.kron(i7, d7))], axis=1)
    fine = to_bf16(np.concatenate([div_i, div_jk], axis=0))
    lift = to_bf16(kron3(up, up, up))
    project = split_columns(kron3(down, down, down))
    mortar_up = np.asarray(np.kron(up, up), np.float32).astype(np.float64)
    mortar_down = np.asarray(np.kron(down, down), np.float32).astype(np.float64)
    selectors = face_selectors(P3)
    raise_faces = split_columns(
        np.concatenate([mortar_up @ selectors[side] for side in range(6)], axis=0)
    )
    lower_faces = split_columns(
        np.concatenate([selectors[side].T @ mortar_down for side in range(6)], axis=1)
    )
    coarse = to_bf16(
        np.concatenate([kron3(d3, i3, i3), kron3(i3, d3, i3), kron3(i3, i3, d3)], axis=1)
    )
    return fine, lift, project, raise_faces, lower_faces, coarse


def dot(a, b):
    return jnp.dot(a, b, preferred_element_type=F32)


def split_rows(value):
    high = value.astype(BF16)
    low = (value - high.astype(F32)).astype(BF16)
    return jnp.concatenate([high, high, low], axis=0)


def face_slices(side):
    dim, end = side // 2, side % 2
    if dim == 0:
        return [pl.ds(448 * end, 64)]
    if dim == 1:
        return [pl.ds(i * 64 + 56 * end, 8) for i in range(P7)]
    return [pl.ds(7 * end, 64, stride=8)]


def face_get(ref, side):
    parts = [ref[where, :] for where in face_slices(side)]
    return parts[0] if len(parts) == 1 else jnp.concatenate(parts, axis=0)


def face_add(ref, side, value):
    start = 0
    for where in face_slices(side):
        ref[where, :] += value[start : start + where.size]
        start += where.size


def kernel(
    slabs,
    pieces,
    state_h,
    vel_h,
    nbr_h,
    pre_h,
    stoich_h,
    switch_h,
    owner_h,
    fine_h,
    lift_h,
    project_h,
    raise_h,
    lower_h,
    coarse_h,
    out7_h,
    out3_h,
    state_v,
    vel_v,
    nbr_v,
    pre_s,
    stoich_s,
    switch_s,
    owner_s,
    fine_v,
    lift_v,
    project_v,
    raise_v,
    lower_v,
    coarse_v,
    u0,
    u1,
    u2,
    u3,
    speed,
    coef,
    vel_rep,
    vmin,
    perm_x,
    perm_o,
    local_nb,
    send,
    recv,
    count_send,
    count_recv,
    home,
    move_send,
    move_recv,
    out7_v,
    out3_v,
    turned,
    home_list,
    load_sem,
    send_sem,
    recv_sem,
    count_ssem,
    count_rsem,
    move_ssem,
    move_rsem,
    store_sem,
):
    slab, pos = lax.axis_index("slab"), lax.axis_index("curve")
    left, right = lax.rem(pos + pieces - 1, pieces), lax.rem(pos + 1, pieces)
    below, above = lax.rem(slab + slabs - 1, slabs), lax.rem(slab + 1, slabs)
    partner = {0: (slab, left), 1: (slab, right), 4: (below, pos), 5: (above, pos)}

    barrier = pltpu.get_barrier_semaphore()
    for side in (0, 1, 4, 5):
        pl.semaphore_signal(barrier, inc=1, device_id=partner[side], device_id_type=MESH)

    pairs = [
        (state_h, state_v),
        (vel_h, vel_v),
        (nbr_h, nbr_v),
        (lift_h, lift_v),
        (pre_h, pre_s),
        (stoich_h, stoich_s),
        (switch_h, switch_s),
        (owner_h, owner_s),
        (fine_h, fine_v),
        (raise_h, raise_v),
        (project_h, project_v),
        (lower_h, lower_v),
        (coarse_h, coarse_v),
    ]
    loads = [
        pltpu.make_async_copy(source, target, load_sem.at[number])
        for number, (source, target) in enumerate(pairs)
    ]
    for load in loads:
        load.start()

    lane_row = lax.broadcasted_iota(jnp.int32, (1, LANES), 1)
    lane_elem = lane_row // FIELDS
    lane_field = lane_row % FIELDS
    lanes = lax.broadcasted_iota(jnp.int32, (LANES, LANES), 1)
    rows = lax.broadcasted_iota(jnp.int32, (LANES, LANES), 0)
    spread = (
        lax.broadcasted_iota(jnp.int32, (ELEMS, LANES), 0)
        == lax.broadcasted_iota(jnp.int32, (ELEMS, LANES), 1) // FIELDS
    ).astype(F32)
    rep = ((rows % FIELDS == 0) & (rows // FIELDS == lanes // FIELDS)).astype(F32).astype(BF16)
    rep2 = jnp.concatenate([rep, rep], axis=0)

    loads[0].wait()
    u0[...] = jnp.transpose(state_v[...].reshape(LANES, 512))

    loads[2].wait()
    ids = nbr_v[...]
    me = slab * pieces + pos
    here = lax.shift_right_logical(ids, 4) == me
    code = jnp.where(here, ids & 15, (ids & 15) + 16).astype(F32)
    spread_t = (
        lax.broadcasted_iota(jnp.int32, (LANES, ELEMS), 1)
        == lax.broadcasted_iota(jnp.int32, (LANES, ELEMS), 0) // FIELDS
    ).astype(F32)
    target = dot(spread_t.astype(BF16), code.astype(BF16)).astype(jnp.int32) * FIELDS
    target = target + lax.broadcasted_iota(jnp.int32, (LANES, 6), 0) % FIELDS
    for side in range(6):
        column = target[:, side : side + 1]
        near = (column == lanes).astype(F32).astype(BF16)
        far = (column == lanes + LANES).astype(F32).astype(BF16)
        if side < 2:
            perm_x[side, :, :LANES] = far
            perm_x[side, :, LANES:] = near
        else:
            perm_o[side - 2] = near if side < 4 else far

    def post(number, traces):
        copies = []
        for side in (0, 1, 4, 5):
            if side < 2:
                both = dot(traces[side], perm_x[side])
                send[number, side] = both[:, :LANES].astype(BF16)
                local_nb[side ^ 1] = both[:, LANES:]
                slot = side
            else:
                slot = side - 2
                send[number, slot] = dot(traces[side], perm_o[side - 2]).astype(BF16)
            copy = pltpu.make_async_remote_copy(
                src_ref=send.at[number, slot],
                dst_ref=recv.at[number, slot ^ 1],
                send_sem=send_sem.at[number, slot],
                recv_sem=recv_sem.at[number, slot ^ 1],
                device_id=partner[side],
                device_id_type=MESH,
            )
            copy.start()
            copies.append(copy)
        for side in (2, 3):
            local_nb[side ^ 1] = dot(traces[side], perm_o[side - 2])
        return copies

    def fine_traces(ref):
        return [face_get(ref, side).astype(BF16) for side in range(6)]

    traces = fine_traces(u0)
    pl.semaphore_wait(barrier, 4)
    copies = post(0, traces)

    loads[6].wait()
    loads[7].wait()
    left_count = right_count = home_count = jnp.int32(0)
    left_pick = [jnp.int32(0)] * 2
    right_pick = [jnp.int32(0)] * 2
    home_pick = [jnp.int32(0)] * HOLD7
    switch_row = jnp.zeros((1, LANES), F32)
    for elem in range(ELEMS):
        switched = switch_s[elem]
        owner = owner_s[elem]
        switch_row = jnp.where(lane_elem == elem, switched.astype(F32), switch_row)
        fine_one = switched != 1
        goes_left = fine_one & (owner == left)
        goes_right = fine_one & (owner == right)
        stays = fine_one & jnp.logical_not(owner == left) & jnp.logical_not(owner == right)
        for slot in range(2):
            left_pick[slot] = jnp.where(goes_left & (left_count == slot), elem, left_pick[slot])
            right_pick[slot] = jnp.where(goes_right & (right_count == slot), elem, right_pick[slot])
        for slot in range(min(elem + 1, HOLD7)):
            home_pick[slot] = jnp.where(stays & (home_count == slot), elem, home_pick[slot])
        left_count = left_count + goes_left.astype(jnp.int32)
        right_count = right_count + goes_right.astype(jnp.int32)
        home_count = home_count + stays.astype(jnp.int32)
    for slot in range(HOLD7):
        home_list[slot] = home_pick[slot]
    count_send[0] = jnp.full((8, LANES), left_count, jnp.int32)
    count_send[1] = jnp.full((8, LANES), right_count, jnp.int32)
    for side in (0, 1):
        copy = pltpu.make_async_remote_copy(
            src_ref=count_send.at[side],
            dst_ref=count_recv.at[side ^ 1],
            send_sem=count_ssem.at[side],
            recv_sem=count_rsem.at[side ^ 1],
            device_id=partner[side],
            device_id_type=MESH,
        )
        copy.start()
        copies.append(copy)
    is_switched = switch_row > 0.5

    loads[1].wait()
    loads[3].wait()
    loads[9].wait()
    for dim in range(3):
        spread_vel = dot(vel_v[dim], spread.astype(BF16)).astype(BF16)
        vel_rep[dim * 64 : dim * 64 + 64] = spread_vel.astype(F32)
        speed[dim] = dot(lift_v[...], spread_vel).astype(BF16).astype(F32)
        mortar = dot(raise_v[dim * 128 : dim * 128 + 128, :128], jnp.concatenate([spread_vel, spread_vel], axis=0))
        vmin[dim * 128 : dim * 128 + 64] = jnp.minimum(-mortar[:64], 0.0)
        vmin[dim * 128 + 64 : dim * 128 + 128] = jnp.minimum(mortar[64:], 0.0)
        for end in range(2):
            side = 2 * dim + end
            normal = face_get(speed.at[dim], side)
            lift_coef = STEP * (P7 * (P7 - 1) / 2.0)
            coef[side] = lift_coef * jnp.minimum(normal if end else -normal, 0.0)

    loads[4].wait()
    loads[5].wait()
    pre_row = jnp.zeros((1, LANES), F32)
    stoich_row = jnp.zeros((1, LANES), F32)
    for elem in range(ELEMS):
        pre_row = jnp.where(lane_elem == elem, pre_s[elem], pre_row)
    for field in range(FIELDS):
        stoich_row = jnp.where(lane_field == field, stoich_s[field], stoich_row)

    def source(u):
        rate = (
            pre_row
            * jnp.exp(-ACTIVATION * jnp.exp(-u))
            * pltpu.roll(u, LANES - 1, 1)
            * pltpu.roll(u, LANES - 2, 1)
        )
        high = rate.astype(BF16)
        low = (rate - high.astype(F32)).astype(BF16)
        return stoich_row * dot(jnp.concatenate([high, low], axis=1), rep2)

    for number in range(8, 13):
        if number != 9:
            loads[number].wait()

    def fine_start(ref, start, out, traces):
        scale = 1.0 if start is None else 0.5
        along_i = []
        for half in range(2):
            parts = []
            for i in range(P7):
                at = pl.ds(i * 64 + half * 32, 32)
                parts.append((speed[0, at, :] * ref[at, :]).astype(BF16))
            along_i.append(dot(fine_v[:256, :], jnp.concatenate(parts, axis=0)))
        for block in range(4):
            at = pl.ds(block * 128, 128)
            u = ref[at, :]
            flux = jnp.concatenate(
                [(speed[1, at, :] * u).astype(BF16), (speed[2, at, :] * u).astype(BF16)], axis=0
            )
            div = dot(fine_v[256:, :], flux) + jnp.concatenate(
                [
                    along_i[half][i * 32 : i * 32 + 32]
                    for i in (2 * block, 2 * block + 1)
                    for half in range(2)
                ],
                axis=0,
            )
            rate = STEP * (source(u) - div)
            out[at, :] = u + rate if start is None else 0.5 * (start[at, :] + u + rate)
        for side in range(6):
            jump = traces[side].astype(F32)
            if side < 4:
                jump = jump - local_nb[side]
            face_add(out, side, scale * (coef[side] * jump))

    def fine_end(number, copies, start, out):
        scale = 1.0 if start is None else 0.5
        for copy in copies:
            copy.wait()
        for side in (0, 1, 4, 5):
            slot = side if side < 2 else side - 2
            face_add(out, side, -scale * (coef[side] * recv[number, slot].astype(F32)))

    def coarse_traces(c):
        return dot(raise_v[...], split_rows(c))

    def coarse_start(c, start):
        flux = jnp.concatenate(
            [(vel_rep[dim * 64 : dim * 64 + 64] * c).astype(BF16) for dim in range(3)], axis=0
        )
        rate = STEP * (source(c) - dot(coarse_v[...], flux))
        return c + rate if start is None else 0.5 * (start + c + rate)

    def coarse_end(number, own, start, partial):
        scale = 1.0 if start is None else 0.5
        jumps = []
        for side in range(6):
            near = None
            if side < 4:
                near = local_nb[side]
            if side not in (2, 3):
                far = recv[number, side if side < 2 else side - 2].astype(F32)
                near = far if near is None else near + far
            mine = own[side * 64 : side * 64 + 64].astype(F32)
            jumps.append(vmin[side * 64 : side * 64 + 64] * (mine - near))
        lift_coef = scale * STEP * (P3 * (P3 - 1) / 2.0)
        return partial + lift_coef * dot(lower_v[...], split_rows(jnp.concatenate(jumps, axis=0)))

    def mixed(fine, raised):
        return [
            jnp.where(is_switched, raised[side * 64 : side * 64 + 64], fine[side].astype(F32)).astype(BF16)
            for side in range(6)
        ]

    fine_start(u0, None, u1, traces)
    fine_end(0, copies, None, u1)
    traces = fine_traces(u1)
    copies = post(1, traces)
    fine_start(u1, u0, u2, traces)
    fine_end(1, copies, u0, u2)

    c0 = dot(project_v[...], split_rows(u2[...]))
    traces = fine_traces(u2)
    raised = coarse_traces(c0)
    copies = post(2, mixed(traces, raised))
    own = raised.astype(BF16)
    fine_start(u2, None, u3, traces)
    partial = coarse_start(c0, None)
    fine_end(2, copies, None, u3)
    c1 = coarse_end(2, own, None, partial)
    traces = fine_traces(u3)
    raised = coarse_traces(c1)
    copies = post(3, mixed(traces, raised))
    own = raised.astype(BF16)
    fine_start(u3, u2, u1, traces)
    partial = coarse_start(c1, c0)
    fine_end(3, copies, u2, u1)

    for number in range(4):
        home[:, :, number * 128 : number * 128 + 128] = jnp.transpose(
            u1[number * 128 : number * 128 + 128, :]
        ).reshape(ELEMS, FIELDS, 128)
    copies = []
    for side in range(2):
        for slot in range(2):
            pick = (left_pick, right_pick)[side][slot]
            move_send[side, slot] = home[pick]
        copy = pltpu.make_async_remote_copy(
            src_ref=move_send.at[side],
            dst_ref=move_recv.at[side ^ 1],
            send_sem=move_ssem.at[side],
            recv_sem=move_rsem.at[side ^ 1],
            device_id=partner[side],
            device_id_type=MESH,
        )
        copy.start()
        copies.append(copy)

    c2 = coarse_end(3, own, c0, partial)
    c2 = jnp.where(is_switched, c2, 0.0)
    turned[...] = jnp.transpose(jnp.concatenate([c2, pltpu.roll(c2, LANES - 1, 1)], axis=0))
    for pair in range(4):
        out3_v[:, pair * 128 : pair * 128 + 128] = turned[pl.ds(2 * pair, ELEMS, stride=FIELDS), :]
    store3 = pltpu.make_async_copy(out3_v, out3_h, store_sem.at[0])
    store3.start()

    from_left = count_recv[0][0, 0]
    from_right = count_recv[1][0, 0]
    is_first, is_last = pos == 0, pos == pieces - 1
    at_left = jnp.where(is_first, home_count + from_right, jnp.where(is_last, from_right, 0))
    at_home = jnp.where(is_first, 0, jnp.where(is_last, from_right + from_left, from_left))
    at_right = jnp.where(is_first, home_count, jnp.where(is_last, 0, from_left + home_count))
    picks = []
    for slot in range(HOLD7):
        rank = slot - at_home
        stay = (rank >= 0) & (rank < home_count)
        value = home[home_list[jnp.clip(rank, 0, HOLD7 - 1)]]
        out7_v[slot] = jnp.where(stay, value, 0.0)
        rank_left, rank_right = slot - at_left, slot - at_right
        is_left = (rank_left >= 0) & (rank_left < from_left)
        is_right = (rank_right >= 0) & (rank_right < from_right)
        pick = jnp.where(is_left, rank_left, jnp.where(is_right, 2 + rank_right, 0))
        picks.append((is_left | is_right, pick))
    for copy in copies:
        copy.wait()
    for slot in range(HOLD7):
        arrived, pick = picks[slot]
        value = move_recv[pick // 2, pick % 2]
        out7_v[slot] = jnp.where(arrived, value, out7_v[slot])
    store7 = pltpu.make_async_copy(out7_v, out7_h, store_sem.at[1])
    store7.start()
    store3.wait()
    store7.wait()


def solution(mesh):
    slabs, pieces = mesh.shape["slab"], mesh.shape["curve"]
    tables = make_tables()

    def per_device(state, velocity, pre_exp, stoich, neighbours, switch, new_owner):
        operands = (state, velocity, neighbours, pre_exp, stoich, switch, new_owner) + tuple(
            jnp.asarray(table) for table in tables
        )
        vm, sm, dma = pltpu.VMEM, pltpu.SMEM, pltpu.SemaphoreType.DMA
        nodes = (512, LANES)
        return pl.pallas_call(
            functools.partial(kernel, slabs, pieces),
            out_shape=(
                jax.ShapeDtypeStruct((HOLD7, FIELDS, 512), F32),
                jax.ShapeDtypeStruct((ELEMS, 512), F32),
            ),
            in_specs=[pl.BlockSpec(memory_space=pl.ANY)] * len(operands),
            out_specs=[pl.BlockSpec(memory_space=pl.ANY)] * 2,
            scratch_shapes=[
                vm((ELEMS, FIELDS, 512), F32),
                vm((3, 64, ELEMS), BF16),
                vm((ELEMS, 6), jnp.int32),
                sm((ELEMS,), F32),
                sm((FIELDS,), F32),
                sm((ELEMS,), jnp.int32),
                sm((ELEMS,), jnp.int32),
            ]
            + [vm(table.shape, BF16) for table in tables]
            + [
                vm(nodes, F32),
                vm(nodes, F32),
                vm(nodes, F32),
                vm(nodes, F32),
                vm((3, 512, LANES), F32),
                vm((6, 64, LANES), F32),
                vm((192, LANES), F32),
                vm((384, LANES), F32),
                vm((2, LANES, 2 * LANES), BF16),
                vm((4, LANES, LANES), BF16),
                vm((4, 64, LANES), F32),
                vm((4, 4, 64, LANES), BF16),
                vm((4, 4, 64, LANES), BF16),
                vm((2, 8, LANES), jnp.int32),
                vm((2, 8, LANES), jnp.int32),
                vm((ELEMS, FIELDS, 512), F32),
                vm((2, 2, FIELDS, 512), F32),
                vm((2, 2, FIELDS, 512), F32),
                vm((HOLD7, FIELDS, 512), F32),
                vm((ELEMS, 512), F32),
                vm((LANES, LANES), F32),
                sm((HOLD7,), jnp.int32),
                dma((13,)),
                dma((4, 4)),
                dma((4, 4)),
                dma((2,)),
                dma((2,)),
                dma((2,)),
                dma((2,)),
                dma((2,)),
            ],
            compiler_params=pltpu.CompilerParams(
                collective_id=0, has_side_effects=True, vmem_limit_bytes=40 * 2**20
            ),
        )(*operands)

    return jax.shard_map(
        per_device,
        mesh=mesh,
        in_specs=(
            P(("slab", "curve"), None, None),
            P(None, None, ("slab", "curve")),
            P(("slab", "curve")),
            P(),
            P(("slab", "curve"), None),
            P(("slab", "curve")),
            P(("slab", "curve")),
        ),
        out_specs=(P(("slab", "curve"), None, None), P(("slab", "curve"), None)),
        check_vma=False,
    )
```

profile of v0, /device:TPU:31, one launch (start us, length us, event | category | flops | bytes accessed | tf_op | source)
XLA Modules:
  0.0 43.2 jit_solution(9237110546374550932)
XLA Ops:
  0.6 0.0 copy-start.11
  0.6 0.8 %copy.16.nbr_h = s32[16,6]{1,0:T(8,128)S(1)} copy(s32[16,6]{0,1:T(8,128)} %param.17) | data formatting | bytes 768 | tf_op args[4]
  1.4 0.0 copy-done.11
  1.4 0.0 copy-start.6
  1.4 0.0 copy-start.7
  1.4 0.0 copy-start.8
  1.4 0.0 copy-start.9
  1.4 0.0 copy-start.10
  1.4 0.1 copy.15.vel_h
  1.6 0.6 %copy-done.6 = bf16[64,192]{1,0:T(8,128)(2,1)S(1)} copy-done((bf16[64,192]{1,0:T(8,128)(2,1)S(1)}, bf16[64,192]{1,0:T(8,128)(2,1)}, u32[]{:S(2)}) %copy-start.6) | copy-done | bytes 24600
  2.2 0.0 copy-done.7
  2.2 0.0 copy-done.8
  2.2 0.0 copy-done.9
  2.2 0.0 copy-done.10
  2.2 0.0 copy-start
  2.2 0.9 %copy-done = f32[16,8,512]{2,1,0:T(8,128)S(1)} copy-done((f32[16,8,512]{2,1,0:T(8,128)S(1)}, f32[16,8,512]{2,1,0:T(8,128)}, u32[]{:S(2)}) %copy-start) | copy-done | bytes 262168
  3.1 0.0 copy-start.1
  3.1 0.9 %copy-done.1 = bf16[384,192]{1,0:T(8,128)(2,1)S(1)} copy-done((bf16[384,192]{1,0:T(8,128)(2,1)S(1)}, bf16[384,192]{1,0:T(8,128)(2,1)}, u32[]{:S(2)}) %copy-start.1) | copy-done | bytes 147480
  4.1 0.0 copy-start.2
  4.1 0.9 %copy-done.2 = bf16[64,1536]{1,0:T(8,128)(2,1)S(1)} copy-done((bf16[64,1536]{1,0:T(8,128)(2,1)S(1)}, bf16[64,1536]{1,0:T(8,128)(2,1)}, u32[]{:S(2)}) %copy-start.2) | copy-done | bytes 196632
  5.0 0.0 copy-start.3
  5.0 0.9 %copy-done.3 = bf16[384,256]{1,0:T(8,128)(2,1)S(1)} copy-done((bf16[384,256]{1,0:T(8,128)(2,1)S(1)}, bf16[384,256]{1,0:T(8,128)(2,1)}, u32[]{:S(2)}) %copy-start.3) | copy-done | bytes 196632
  5.9 0.0 copy-start.4
  5.9 0.9 %copy-done.4 = bf16[64,1152]{1,0:T(8,128)(2,1)S(1)} copy-done((bf16[64,1152]{1,0:T(8,128)(2,1)S(1)}, bf16[64,1152]{1,0:T(8,128)(2,1)}, u32[]{:S(2)}) %copy-start.4) | copy-done | bytes 147480
  6.8 0.0 copy-start.5
  6.8 0.9 %copy-done.5 = bf16[512,64]{1,0:T(8,128)(2,1)S(1)} copy-done((bf16[512,64]{1,0:T(8,128)(2,1)S(1)}, bf16[512,64]{1,0:T(8,128)(2,1)}, u32[]{:S(2)}) %copy-start.5) | copy-done | bytes 65560
  7.7 34.2 %shard_map.140 = (f32[12,8,512]{2,1,0:T(8,128)S(1)}, f32[16,512]{1,0:T(8,128)S(1)}) custom-call(f32[16,8,512]{2,1,0:T(8,128)S(1)} %copy-done, bf16[3,64,16]{2,1,0:T(8,128)(2,1)S(1)} %copy.15.vel_h, s32[16,6]{1,0:T(8,128)S(1)} %copy.16.nbr_h, f32[16]{0:T(128)S(1)} %copy-done.7, f32[8]{0:T(128)S(1)} %copy-done.8, s32[16]{0:T(128)S(1)} %copy-done.9, ...), custom_call_target="tpu_custom_call" | custom-call | tf_op jit(solution)/shard_map/pallas_call | solution.py:544
  41.9 0.7 %copy.19 = f32[12,8,512]{2,1,0:T(8,128)} copy(f32[12,8,512]{2,1,0:T(8,128)S(1)} %get-tuple-element.4) | data formatting | bytes 393216
  42.6 0.6 %copy.20 = f32[16,512]{1,0:T(8,128)} copy(f32[16,512]{1,0:T(8,128)S(1)} %get-tuple-element.5) | data formatting | bytes 65536
Async XLA Ops:
  0.6 0.8 %copy-start.11 = (bf16[3,64,16]{1,2,0:T(8,128)(2,1)S(1)}, bf16[3,64,16]{1,2,0:T(8,128)(2,1)}, u32[]{:S(2)}) copy-start(bf16[3,64,16]{1,2,0:T(8,128)(2,1)} %param.14) | copy-start | bytes 18436
  1.4 0.8 %copy-start.6 = (bf16[64,192]{1,0:T(8,128)(2,1)S(1)}, bf16[64,192]{1,0:T(8,128)(2,1)}, u32[]{:S(2)}) copy-start(bf16[64,192]{1,0:T(8,128)(2,1)} %constant.17.clone.coarse_h) | copy-start | bytes 73732
  1.4 0.8 %copy-start.7 = (f32[16]{0:T(128)S(1)}, f32[16]{0:T(128)}, u32[]{:S(2)}) copy-start(f32[16]{0:T(128)} %pre_h.1) | copy-start | bytes 196
  1.4 0.8 %copy-start.8 = (f32[8]{0:T(128)S(1)}, f32[8]{0:T(128)}, u32[]{:S(2)}) copy-start(f32[8]{0:T(128)} %stoich_h.1) | copy-start | bytes 100
  1.4 0.8 %copy-start.9 = (s32[16]{0:T(128)S(1)}, s32[16]{0:T(128)}, u32[]{:S(2)}) copy-start(s32[16]{0:T(128)} %switch_h.1) | copy-start | bytes 196
  1.4 0.7 %copy-start.10 = (s32[16]{0:T(128)S(1)}, s32[16]{0:T(128)}, u32[]{:S(2)}) copy-start(s32[16]{0:T(128)} %owner_h.1) | copy-start | bytes 196
  2.2 1.0 %copy-start = (f32[16,8,512]{2,1,0:T(8,128)S(1)}, f32[16,8,512]{2,1,0:T(8,128)}, u32[]{:S(2)}) copy-start(f32[16,8,512]{2,1,0:T(8,128)} %state_h.1) | copy-start | bytes 786436
  3.1 0.9 %copy-start.1 = (bf16[384,192]{1,0:T(8,128)(2,1)S(1)}, bf16[384,192]{1,0:T(8,128)(2,1)}, u32[]{:S(2)}) copy-start(bf16[384,192]{1,0:T(8,128)(2,1)} %constant.15.clone.raise_h) | copy-start | bytes 442372
  4.1 0.9 %copy-start.2 = (bf16[64,1536]{1,0:T(8,128)(2,1)S(1)}, bf16[64,1536]{1,0:T(8,128)(2,1)}, u32[]{:S(2)}) copy-start(bf16[64,1536]{1,0:T(8,128)(2,1)} %constant.14.clone.project_h) | copy-start | bytes 589828
  5.0 0.9 %copy-start.3 = (bf16[384,256]{1,0:T(8,128)(2,1)S(1)}, bf16[384,256]{1,0:T(8,128)(2,1)}, u32[]{:S(2)}) copy-start(bf16[384,256]{1,0:T(8,128)(2,1)} %constant.12.clone.fine_h) | copy-start | bytes 589828
  5.9 0.9 %copy-start.4 = (bf16[64,1152]{1,0:T(8,128)(2,1)S(1)}, bf16[64,1152]{1,0:T(8,128)(2,1)}, u32[]{:S(2)}) copy-start(bf16[64,1152]{1,0:T(8,128)(2,1)} %constant.16.clone.lower_h) | copy-start | bytes 442372
  6.8 0.9 %copy-start.5 = (bf16[512,64]{1,0:T(8,128)(2,1)S(1)}, bf16[512,64]{1,0:T(8,128)(2,1)}, u32[]{:S(2)}) copy-start(bf16[512,64]{1,0:T(8,128)(2,1)} %constant.13.clone.lift_h) | copy-start | bytes 196612
where the time goes:
time: 43.6 us; the launch traced here: 43.2 us
  Pallas kernels  34.2 us (78%)
  local copies, waits for them, and re-layouts  8.35 us (19%)
  between operations  0.69 us (2%)
    pallas_call x1, Pallas kernels, per_device(): pl.pallas_call(functools.partial(kernel, slabs, pieces), out_shape=(jax.S...  34.2 us
    unnamed x28, local copies, waits for them, and re-layouts  8.35 us

commit v1 on v0

--- a/solution.py
+++ b/solution.py
@@ -256,7 +256,13 @@
         lax.broadcasted_iota(jnp.int32, (LANES, ELEMS), 1)
         == lax.broadcasted_iota(jnp.int32, (LANES, ELEMS), 0) // FIELDS
     ).astype(F32)
-    target = dot(spread_t.astype(BF16), code.astype(BF16)).astype(jnp.int32) * FIELDS
+    target = lax.dot_general(
+        spread_t.astype(BF16),
+        code.astype(BF16),
+        (((1,), (1,)), ((), ())),
+        preferred_element_type=F32,
+    )
+    target = target.astype(jnp.int32) * FIELDS
     target = target + lax.broadcasted_iota(jnp.int32, (LANES, 6), 0) % FIELDS
     for side in range(6):
         column = target[:, side : side + 1]
@@ -344,7 +350,12 @@
     loads[3].wait()
     loads[9].wait()
     for dim in range(3):
-        spread_vel = dot(vel_v[dim], spread.astype(BF16)).astype(BF16)
+        spread_vel = lax.dot_general(
+            vel_v[dim],
+            spread.astype(BF16),
+            (((0,), (0,)), ((), ())),
+            preferred_element_type=F32,
+        ).astype(BF16)
         vel_rep[dim * 64 : dim * 64 + 64] = spread_vel.astype(F32)
         speed[dim] = dot(lift_v[...], spread_vel).astype(BF16).astype(F32)
         mortar = dot(raise_v[dim * 128 : dim * 128 + 128, :128], jnp.concatenate([spread_vel, spread_vel], axis=0))
@@ -502,8 +513,8 @@
     store3 = pltpu.make_async_copy(out3_v, out3_h, store_sem.at[0])
     store3.start()
 
-    from_left = count_recv[0][0, 0]
-    from_right = count_recv[1][0, 0]
+    from_left = jnp.minimum(count_recv[0][0, 0], 2)
+    from_right = jnp.minimum(count_recv[1][0, 0], 2)
     is_first, is_last = pos == 0, pos == pieces - 1
     at_left = jnp.where(is_first, home_count + from_right, jnp.where(is_last, from_right, 0))
     at_home = jnp.where(is_first, 0, jnp.where(is_last, from_right + from_left, from_left))
@@ -536,6 +547,8 @@
     tables = make_tables()
 
     def per_device(state, velocity, pre_exp, stoich, neighbours, switch, new_owner):
+        velocity = jnp.transpose(velocity, (0, 2, 1))
+        neighbours = jnp.transpose(neighbours)
         operands = (state, velocity, neighbours, pre_exp, stoich, switch, new_owner) + tuple(
             jnp.asarray(table) for table in tables
         )
@@ -547,12 +560,12 @@
                 jax.ShapeDtypeStruct((HOLD7, FIELDS, 512), F32),
                 jax.ShapeDtypeStruct((ELEMS, 512), F32),
             ),
-            in_specs=[pl.BlockSpec(memory_space=pl.ANY)] * len(operands),
-            out_specs=[pl.BlockSpec(memory_space=pl.ANY)] * 2,
+            in_specs=[pl.BlockSpec(memory_space=pltpu.HBM)] * len(operands),
+            out_specs=[pl.BlockSpec(memory_space=pltpu.HBM)] * 2,
             scratch_shapes=[
                 vm((ELEMS, FIELDS, 512), F32),
-                vm((3, 64, ELEMS), BF16),
-                vm((ELEMS, 6), jnp.int32),
+                vm((3, ELEMS, 64), BF16),
+                vm((6, ELEMS), jnp.int32),
                 sm((ELEMS,), F32),
                 sm((FIELDS,), F32),
                 sm((ELEMS,), jnp.int32),
@@ -592,7 +605,7 @@
                 dma((2,)),
             ],
             compiler_params=pltpu.CompilerParams(
-                collective_id=0, has_side_effects=True, vmem_limit_bytes=40 * 2**20
+                collective_id=0, has_side_effects=True, vmem_limit_bytes=63 * 2**20
             ),
         )(*operands)
 

time: 43.6 us -> 37.6 us (0.86)
  local copies, waits for them, and re-layouts: 8.35 us -> 2.24 us
    unnamed x28 -> x4, local copies, waits for them, and re-layouts: 8.35 us -> 2.24 us
where the time goes in v1:
time: 37.6 us; the launch traced here: 37.4 us
  Pallas kernels  34.5 us (92%)
  local copies, waits for them, and re-layouts  2.24 us (6%)
  between operations  0.65 us (2%)
    pallas_call x1, Pallas kernels, per_device(): pl.pallas_call(functools.partial(kernel, slabs, pieces), out_shape=(jax.S...  34.5 us
    unnamed x4, local copies, waits for them, and re-layouts  2.24 us

profile of v1, /device:TPU:31, one launch (start us, length us, event | category | flops | bytes accessed | tf_op | source)
XLA Modules:
  0.0 37.4 jit_solution(9231717841388330050)
XLA Ops:
  0.6 34.5 %shard_map.140 = (f32[12,8,512]{2,1,0:T(8,128)}, f32[16,512]{1,0:T(8,128)}) custom-call(f32[16,8,512]{2,1,0:T(8,128)} %state_h.1, bf16[3,16,64]{2,1,0:T(8,128)(2,1)} %bitcast.2, s32[6,16]{1,0:T(8,128)} %bitcast.3, f32[16]{0:T(128)} %pre_h.1, f32[8]{0:T(128)} %stoich_h.1, s32[16]{0:T(128)} %switch_h.1, s32[16]{0:T(128)} %owner_h.1, ...), custom_call_target="tpu_custom_call" | custom-call | tf_op jit(solution)/shard_map/pallas_call | solution.py:557
  35.2 0.0 copy-start
  35.2 1.6 %copy.17 = f32[12,8,512]{2,1,0:T(8,128)} copy(f32[12,8,512]{2,1,0:T(8,128)} %get-tuple-element.4) | data formatting | bytes 393216
  36.8 0.0 copy-done
  36.8 0.6 %copy.18 = f32[16,512]{1,0:T(8,128)} copy(f32[16,512]{1,0:T(8,128)S(1)} %copy-done) | data formatting | bytes 65536
Async XLA Ops:
  35.2 1.6 %copy-start = (f32[16,512]{1,0:T(8,128)S(1)}, f32[16,512]{1,0:T(8,128)}, u32[]{:S(2)}) copy-start(f32[16,512]{1,0:T(8,128)} %get-tuple-element.5) | copy-start | bytes 98308

commit v2 on v1

--- a/solution.py
+++ b/solution.py
@@ -96,16 +96,20 @@
     mortar_up = np.asarray(np.kron(up, up), np.float32).astype(np.float64)
     mortar_down = np.asarray(np.kron(down, down), np.float32).astype(np.float64)
     selectors = face_selectors(P3)
-    raise_faces = split_columns(
-        np.concatenate([mortar_up @ selectors[side] for side in range(6)], axis=0)
-    )
-    lower_faces = split_columns(
-        np.concatenate([selectors[side].T @ mortar_down for side in range(6)], axis=1)
-    )
+    raise_all = np.concatenate([mortar_up @ selectors[side] for side in range(6)], axis=0)
+    lower_all = np.concatenate([selectors[side].T @ mortar_down for side in range(6)], axis=1)
+    lower_all = STEP * (P3 * (P3 - 1) / 2.0) * lower_all
+    raise_faces = split_columns(raise_all)
+    lower_faces = split_columns(lower_all)
+    project_all = np.asarray(kron3(down, down, down), np.float32).astype(np.float64)
+    project_x = np.concatenate([project_all[:, :64], project_all[:, 448:]], axis=1)
+    late_fine = split_columns(np.concatenate([raise_all @ project_x, project_x], axis=0))
+    lower_x = lower_all[:, :128]
+    late_coarse = split_columns(np.concatenate([raise_all @ lower_x, lower_x], axis=0))
     coarse = to_bf16(
         np.concatenate([kron3(d3, i3, i3), kron3(i3, d3, i3), kron3(i3, i3, d3)], axis=1)
     )
-    return fine, lift, project, raise_faces, lower_faces, coarse
+    return fine, lift, project, raise_faces, lower_faces, coarse, late_fine, late_coarse
 
 
 def dot(a, b):
@@ -155,8 +159,10 @@
     raise_h,
     lower_h,
     coarse_h,
-    out7_h,
-    out3_h,
+    late_fine_h,
+    late_coarse_h,
+    out7_v,
+    out3_v,
     state_v,
     vel_v,
     nbr_v,
@@ -170,6 +176,8 @@
     raise_v,
     lower_v,
     coarse_v,
+    late_fine_v,
+    late_coarse_v,
     u0,
     u1,
     u2,
@@ -178,8 +186,8 @@
     coef,
     vel_rep,
     vmin,
-    perm_x,
-    perm_o,
+    perm_far,
+    perm_near,
     local_nb,
     send,
     recv,
@@ -188,8 +196,10 @@
     home,
     move_send,
     move_recv,
-    out7_v,
-    out3_v,
+    early_send,
+    early_recv,
+    extra_recv,
+    move_coef,
     turned,
     home_list,
     load_sem,
@@ -199,7 +209,10 @@
     count_rsem,
     move_ssem,
     move_rsem,
-    store_sem,
+    early_ssem,
+    early_rsem,
+    extra_ssem,
+    extra_rsem,
 ):
     slab, pos = lax.axis_index("slab"), lax.axis_index("curve")
     left, right = lax.rem(pos + pieces - 1, pieces), lax.rem(pos + 1, pieces)
@@ -224,6 +237,8 @@
         (project_h, project_v),
         (lower_h, lower_v),
         (coarse_h, coarse_v),
+        (late_fine_h, late_fine_v),
+        (late_coarse_h, late_coarse_v),
     ]
     loads = [
         pltpu.make_async_copy(source, target, load_sem.at[number])
@@ -269,42 +284,42 @@
         near = (column == lanes).astype(F32).astype(BF16)
         far = (column == lanes + LANES).astype(F32).astype(BF16)
         if side < 2:
-            perm_x[side, :, :LANES] = far
-            perm_x[side, :, LANES:] = near
+            perm_far[side] = far
+            perm_near[side] = near
+        elif side < 4:
+            perm_near[side] = near
         else:
-            perm_o[side - 2] = near if side < 4 else far
-
-    def post(number, traces):
-        copies = []
-        for side in (0, 1, 4, 5):
-            if side < 2:
-                both = dot(traces[side], perm_x[side])
-                send[number, side] = both[:, :LANES].astype(BF16)
-                local_nb[side ^ 1] = both[:, LANES:]
-                slot = side
-            else:
-                slot = side - 2
-                send[number, slot] = dot(traces[side], perm_o[side - 2]).astype(BF16)
-            copy = pltpu.make_async_remote_copy(
-                src_ref=send.at[number, slot],
-                dst_ref=recv.at[number, slot ^ 1],
-                send_sem=send_sem.at[number, slot],
-                recv_sem=recv_sem.at[number, slot ^ 1],
-                device_id=partner[side],
-                device_id_type=MESH,
-            )
-            copy.start()
-            copies.append(copy)
-        for side in (2, 3):
-            local_nb[side ^ 1] = dot(traces[side], perm_o[side - 2])
-        return copies
-
-    def fine_traces(ref):
-        return [face_get(ref, side).astype(BF16) for side in range(6)]
-
-    traces = fine_traces(u0)
+            perm_far[side - 2] = far
+
+    def launch(number, side, trace):
+        slot = side if side < 2 else side - 2
+        send[number, slot] = dot(trace, perm_far[slot]).astype(BF16)
+        copy = pltpu.make_async_remote_copy(
+            src_ref=send.at[number, slot],
+            dst_ref=recv.at[number, slot ^ 1],
+            send_sem=send_sem.at[number, slot],
+            recv_sem=recv_sem.at[number, slot ^ 1],
+            device_id=partner[side],
+            device_id_type=MESH,
+        )
+        copy.start()
+        started.append(copy)
+        arrivals[number, side ^ 1] = copy
+
+    def gather_local(traces):
+        for side in range(4):
+            local_nb[side ^ 1] = dot(traces[side], perm_near[side])
+
+    started, arrivals = [], {}
+
+    def fine_trace(ref, side):
+        return face_get(ref, side).astype(BF16)
+
+    traces = [fine_trace(u0, side) for side in range(6)]
     pl.semaphore_wait(barrier, 4)
-    copies = post(0, traces)
+    for side in (0, 1, 4, 5):
+        launch(0, side, traces[side])
+    gather_local(traces)
 
     loads[6].wait()
     loads[7].wait()
@@ -331,6 +346,7 @@
         home_count = home_count + stays.astype(jnp.int32)
     for slot in range(HOLD7):
         home_list[slot] = home_pick[slot]
+    count_arrivals = []
     count_send[0] = jnp.full((8, LANES), left_count, jnp.int32)
     count_send[1] = jnp.full((8, LANES), right_count, jnp.int32)
     for side in (0, 1):
@@ -343,7 +359,8 @@
             device_id_type=MESH,
         )
         copy.start()
-        copies.append(copy)
+        started.append(copy)
+        count_arrivals.append(copy)
     is_switched = switch_row > 0.5
 
     loads[1].wait()
@@ -367,6 +384,30 @@
             lift_coef = STEP * (P7 * (P7 - 1) / 2.0)
             coef[side] = lift_coef * jnp.minimum(normal if end else -normal, 0.0)
 
+    for side, picks, count in ((0, left_pick, left_count), (1, right_pick, right_count)):
+        chosen = jnp.zeros((LANES, LANES), F32)
+        for slot in range(2):
+            place = lanes // FIELDS == 2 * (1 - side) + slot
+            source_row = rows - (lanes % FIELDS) == picks[slot] * FIELDS
+            chosen = jnp.where(place & source_row & (count > slot), 1.0, chosen)
+        chosen = chosen.astype(BF16)
+        early_send[side, :LANES] = chosen
+        normals = jnp.concatenate(
+            [face_get(speed.at[other // 2], other).astype(BF16) for other in (0, 1, 4, 5)], axis=0
+        )
+        early_send[side, LANES:] = dot(normals, chosen).astype(BF16)
+        copy = pltpu.make_async_remote_copy(
+            src_ref=early_send.at[side],
+            dst_ref=early_recv.at[side ^ 1],
+            send_sem=early_ssem.at[side],
+            recv_sem=early_rsem.at[side ^ 1],
+            device_id=partner[side],
+            device_id_type=MESH,
+        )
+        copy.start()
+        started.append(copy)
+        count_arrivals.append(copy)
+
     loads[4].wait()
     loads[5].wait()
     pre_row = jnp.zeros((1, LANES), F32)
@@ -387,7 +428,7 @@
         low = (rate - high.astype(F32)).astype(BF16)
         return stoich_row * dot(jnp.concatenate([high, low], axis=1), rep2)
 
-    for number in range(8, 13):
+    for number in range(8, 15):
         if number != 9:
             loads[number].wait()
 
@@ -422,16 +463,20 @@
                 jump = jump - local_nb[side]
             face_add(out, side, scale * (coef[side] * jump))
 
-    def fine_end(number, copies, start, out):
-        scale = 1.0 if start is None else 0.5
-        for copy in copies:
-            copy.wait()
-        for side in (0, 1, 4, 5):
-            slot = side if side < 2 else side - 2
-            face_add(out, side, -scale * (coef[side] * recv[number, slot].astype(F32)))
-
-    def coarse_traces(c):
-        return dot(raise_v[...], split_rows(c))
+    def late_term(number, side, scale):
+        slot = side if side < 2 else side - 2
+        arrivals[number, side].wait_recv()
+        return scale * (coef[side] * recv[number, slot].astype(F32))
+
+    def fine_end_z(number, scale, out):
+        for side in (4, 5):
+            face_add(out, side, -late_term(number, side, scale))
+
+    def fine_end_x(number, scale, out):
+        terms = [late_term(number, side, scale) for side in (0, 1)]
+        for side in (0, 1):
+            face_add(out, side, -terms[side])
+        return jnp.concatenate(terms, axis=0)
 
     def coarse_start(c, start):
         flux = jnp.concatenate(
@@ -440,56 +485,109 @@
         rate = STEP * (source(c) - dot(coarse_v[...], flux))
         return c + rate if start is None else 0.5 * (start + c + rate)
 
-    def coarse_end(number, own, start, partial):
-        scale = 1.0 if start is None else 0.5
+    def coarse_end_z(number, own, scale, partial):
         jumps = []
         for side in range(6):
-            near = None
-            if side < 4:
-                near = local_nb[side]
-            if side not in (2, 3):
-                far = recv[number, side if side < 2 else side - 2].astype(F32)
-                near = far if near is None else near + far
+            near = local_nb[side] if side < 4 else recv[number, side - 2].astype(F32)
             mine = own[side * 64 : side * 64 + 64].astype(F32)
             jumps.append(vmin[side * 64 : side * 64 + 64] * (mine - near))
-        lift_coef = scale * STEP * (P3 * (P3 - 1) / 2.0)
-        return partial + lift_coef * dot(lower_v[...], split_rows(jnp.concatenate(jumps, axis=0)))
-
-    def mixed(fine, raised):
-        return [
-            jnp.where(is_switched, raised[side * 64 : side * 64 + 64], fine[side].astype(F32)).astype(BF16)
-            for side in range(6)
-        ]
+        return partial + scale * dot(lower_v[...], split_rows(jnp.concatenate(jumps, axis=0)))
+
+    def coarse_jump_x(number):
+        return split_rows(
+            jnp.concatenate(
+                [vmin[side * 64 : side * 64 + 64] * recv[number, side].astype(F32) for side in (0, 1)],
+                axis=0,
+            )
+        )
+
+    def launch_mixed(number, fine, raised_base, table, late):
+        own, traces = [None] * 6, [None] * 6
+        for sides in ((0, 1), (4, 5), (2, 3)):
+            at = slice(sides[0] * 64, sides[0] * 64 + 128)
+            raised = raised_base[at] - dot(table[at, :], late)
+            for place, side in enumerate(sides):
+                own[side] = raised[place * 64 : place * 64 + 64]
+                traces[side] = fine_trace(fine, side)
+                mixed = jnp.where(is_switched, own[side], traces[side].astype(F32)).astype(BF16)
+                if side in (2, 3):
+                    mixes[side] = mixed
+                else:
+                    launch(number, side, mixed)
+                    mixes[side] = mixed
+        return traces, jnp.concatenate(own, axis=0).astype(BF16)
+
+    mixes = [None] * 6
 
     fine_start(u0, None, u1, traces)
-    fine_end(0, copies, None, u1)
-    traces = fine_traces(u1)
-    copies = post(1, traces)
+    fine_end_z(0, 1.0, u1)
+    fine_end_x(0, 1.0, u1)
+    traces = [None] * 6
+    for side in (0, 1, 4, 5):
+        traces[side] = fine_trace(u1, side)
+        launch(1, side, traces[side])
+    for side in (2, 3):
+        traces[side] = fine_trace(u1, side)
+    gather_local(traces)
     fine_start(u1, u0, u2, traces)
-    fine_end(1, copies, u0, u2)
-
+    fine_end_z(1, 0.5, u2)
     c0 = dot(project_v[...], split_rows(u2[...]))
-    traces = fine_traces(u2)
-    raised = coarse_traces(c0)
-    copies = post(2, mixed(traces, raised))
-    own = raised.astype(BF16)
+    raised = dot(raise_v[...], split_rows(c0))
+    late = split_rows(fine_end_x(1, 0.5, u2))
+
+    traces, own = launch_mixed(2, u2, raised, late_fine_v, late)
+    gather_local(mixes)
+    c0 = c0 - dot(late_fine_v[384:, :], late)
     fine_start(u2, None, u3, traces)
     partial = coarse_start(c0, None)
-    fine_end(2, copies, None, u3)
-    c1 = coarse_end(2, own, None, partial)
-    traces = fine_traces(u3)
-    raised = coarse_traces(c1)
-    copies = post(3, mixed(traces, raised))
-    own = raised.astype(BF16)
+    for copy in count_arrivals:
+        copy.wait_recv()
+    for place, side in enumerate((0, 1, 4, 5)):
+        at = pl.ds(LANES + 64 * place, 64)
+        normal = early_recv[0, at, :].astype(F32) + early_recv[1, at, :].astype(F32)
+        lift_coef = 0.5 * STEP * (P7 * (P7 - 1) / 2.0)
+        move_coef[place] = lift_coef * jnp.minimum(normal if side % 2 else -normal, 0.0)
+    fine_end_z(2, 1.0, u3)
+    c1 = coarse_end_z(2, own, 1.0, partial)
+    raised = dot(raise_v[...], split_rows(c1))
+    fine_end_x(2, 1.0, u3)
+    late = coarse_jump_x(2)
+    traces, own = launch_mixed(3, u3, raised, late_coarse_v, late)
+
+    left2, right2 = lax.rem(pos + pieces - 2, pieces), lax.rem(pos + 2, pieces)
+    extras = {
+        (1, 1): (2, (below, right)),
+        (1, 2): (3, (above, right)),
+        (0, 1): (2, (below, left)),
+        (0, 2): (3, (above, left)),
+        (0, 0): (0, (slab, left2)),
+        (1, 0): (1, (slab, right2)),
+    }
+    extra_copies = []
+    for (toward, kind), (slot, device) in extras.items():
+        place = 3 - kind if kind else 0
+        copy = pltpu.make_async_remote_copy(
+            src_ref=send.at[3, slot],
+            dst_ref=extra_recv.at[1 - toward, place],
+            send_sem=extra_ssem.at[toward, kind],
+            recv_sem=extra_rsem.at[1 - toward, place],
+            device_id=device,
+            device_id_type=MESH,
+        )
+        copy.start()
+        started.append(copy)
+        extra_copies.append(copy)
+    gather_local(mixes)
+    c1 = c1 - dot(late_coarse_v[384:, :], late)
     fine_start(u3, u2, u1, traces)
-    partial = coarse_start(c1, c0)
-    fine_end(3, copies, u2, u1)
-
-    for number in range(4):
-        home[:, :, number * 128 : number * 128 + 128] = jnp.transpose(
-            u1[number * 128 : number * 128 + 128, :]
-        ).reshape(ELEMS, FIELDS, 128)
-    copies = []
+
+    def turn_home():
+        for number in range(4):
+            home[:, :, number * 128 : number * 128 + 128] = jnp.transpose(
+                u1[number * 128 : number * 128 + 128, :]
+            ).reshape(ELEMS, FIELDS, 128)
+
+    turn_home()
     for side in range(2):
         for slot in range(2):
             pick = (left_pick, right_pick)[side][slot]
@@ -503,15 +601,20 @@
             device_id_type=MESH,
         )
         copy.start()
-        copies.append(copy)
-
-    c2 = coarse_end(3, own, c0, partial)
+        started.append(copy)
+        extra_copies.append(copy)
+    partial = coarse_start(c1, c0)
+    u3[...] = jnp.zeros_like(u3)
+    fine_end_z(3, 0.5, u1)
+    c2 = coarse_end_z(3, own, 0.5, partial)
+    fine_end_x(3, 0.5, u1)
+    c2 = c2 - 0.5 * dot(late_coarse_v[384:, :], coarse_jump_x(3))
+
     c2 = jnp.where(is_switched, c2, 0.0)
     turned[...] = jnp.transpose(jnp.concatenate([c2, pltpu.roll(c2, LANES - 1, 1)], axis=0))
     for pair in range(4):
         out3_v[:, pair * 128 : pair * 128 + 128] = turned[pl.ds(2 * pair, ELEMS, stride=FIELDS), :]
-    store3 = pltpu.make_async_copy(out3_v, out3_h, store_sem.at[0])
-    store3.start()
+    turn_home()
 
     from_left = jnp.minimum(count_recv[0][0, 0], 2)
     from_right = jnp.minimum(count_recv[1][0, 0], 2)
@@ -530,16 +633,29 @@
         is_right = (rank_right >= 0) & (rank_right < from_right)
         pick = jnp.where(is_left, rank_left, jnp.where(is_right, 2 + rank_right, 0))
         picks.append((is_left | is_right, pick))
-    for copy in copies:
-        copy.wait()
+    for copy in extra_copies:
+        copy.wait_recv()
+    chosen = jnp.concatenate([early_recv[0, :LANES, :], early_recv[1, :LANES, :]], axis=0)
+    nears = {
+        0: (extra_recv[0, 0], send[3, 1]),
+        1: (send[3, 0], extra_recv[1, 0]),
+        4: (extra_recv[0, 1], extra_recv[1, 1]),
+        5: (extra_recv[0, 2], extra_recv[1, 2]),
+    }
+    for place, side in enumerate((0, 1, 4, 5)):
+        near = dot(jnp.concatenate(nears[side], axis=1), chosen)
+        face_add(u3, side, -(move_coef[place] * near))
+    for number in range(4):
+        moved = jnp.transpose(u3[number * 128 : number * 128 + 128, :])
+        at = pl.ds(number * 128, 128)
+        for pick in range(4):
+            move_recv[pick // 2, pick % 2, :, at] += moved[pick * FIELDS : pick * FIELDS + FIELDS]
     for slot in range(HOLD7):
         arrived, pick = picks[slot]
         value = move_recv[pick // 2, pick % 2]
         out7_v[slot] = jnp.where(arrived, value, out7_v[slot])
-    store7 = pltpu.make_async_copy(out7_v, out7_h, store_sem.at[1])
-    store7.start()
-    store3.wait()
-    store7.wait()
+    for copy in started:
+        copy.wait_send()
 
 
 def solution(mesh):
@@ -557,11 +673,11 @@
         return pl.pallas_call(
             functools.partial(kernel, slabs, pieces),
             out_shape=(
-                jax.ShapeDtypeStruct((HOLD7, FIELDS, 512), F32),
-                jax.ShapeDtypeStruct((ELEMS, 512), F32),
+                pltpu.VMEM((HOLD7, FIELDS, 512), F32),
+                pltpu.VMEM((ELEMS, 512), F32),
             ),
             in_specs=[pl.BlockSpec(memory_space=pltpu.HBM)] * len(operands),
-            out_specs=[pl.BlockSpec(memory_space=pltpu.HBM)] * 2,
+            out_specs=[pl.BlockSpec(memory_space=pltpu.VMEM)] * 2,
             scratch_shapes=[
                 vm((ELEMS, FIELDS, 512), F32),
                 vm((3, ELEMS, 64), BF16),
@@ -581,7 +697,7 @@
                 vm((6, 64, LANES), F32),
                 vm((192, LANES), F32),
                 vm((384, LANES), F32),
-                vm((2, LANES, 2 * LANES), BF16),
+                vm((4, LANES, LANES), BF16),
                 vm((4, LANES, LANES), BF16),
                 vm((4, 64, LANES), F32),
                 vm((4, 4, 64, LANES), BF16),
@@ -591,11 +707,13 @@
                 vm((ELEMS, FIELDS, 512), F32),
                 vm((2, 2, FIELDS, 512), F32),
                 vm((2, 2, FIELDS, 512), F32),
-                vm((HOLD7, FIELDS, 512), F32),
-                vm((ELEMS, 512), F32),
+                vm((2, 3 * LANES, LANES), BF16),
+                vm((2, 3 * LANES, LANES), BF16),
+                vm((2, 3, 64, LANES), BF16),
+                vm((4, 64, LANES), F32),
                 vm((LANES, LANES), F32),
                 sm((HOLD7,), jnp.int32),
-                dma((13,)),
+                dma((15,)),
                 dma((4, 4)),
                 dma((4, 4)),
                 dma((2,)),
@@ -603,9 +721,12 @@
                 dma((2,)),
                 dma((2,)),
                 dma((2,)),
+                dma((2,)),
+                dma((2, 3)),
+                dma((2, 3)),
             ],
             compiler_params=pltpu.CompilerParams(
-                collective_id=0, has_side_effects=True, vmem_limit_bytes=63 * 2**20
+                collective_id=0, has_side_effects=True, vmem_limit_bytes=62 * 2**20
             ),
         )(*operands)
 

time: 37.6 us -> 34.3 us (0.912)
  the two profiles are of different devices: /device:TPU:31 before, /device:TPU:1 now
where the time goes in v2:
time: 34.3 us; the launch traced here: 34.2 us
  Pallas kernels  32.2 us (94%)
  local copies, waits for them, and re-layouts  1.29 us (4%)
  between operations  0.64 us (2%)
    pallas_call x1, Pallas kernels, per_device(): pl.pallas_call(functools.partial(kernel, slabs, pieces), out_shape=(pltpu...  32.2 us
    unnamed x2, local copies, waits for them, and re-layouts  1.29 us

profile of v2, /device:TPU:1, one launch (start us, length us, event | category | flops | bytes accessed | tf_op | source)
XLA Modules:
  0.0 34.2 jit_solution(11311686811380091748)
XLA Ops:
  0.6 32.2 %shard_map.158 = (f32[12,8,512]{2,1,0:T(8,128)S(1)}, f32[16,512]{1,0:T(8,128)S(1)}) custom-call(f32[16,8,512]{2,1,0:T(8,128)} %state_h.1, bf16[3,16,64]{2,1,0:T(8,128)(2,1)} %bitcast.2, s32[6,16]{1,0:T(8,128)} %bitcast.3, f32[16]{0:T(128)} %pre_h.1, f32[8]{0:T(128)} %stoich_h.1, s32[16]{0:T(128)} %switch_h.1, s32[16]{0:T(128)} %owner_h.1, ...), custom_call_target="tpu_custom_call" | custom-call | tf_op jit(solution)/shard_map/pallas_call | solution.py:673
  32.9 0.7 %copy.19 = f32[12,8,512]{2,1,0:T(8,128)} copy(f32[12,8,512]{2,1,0:T(8,128)S(1)} %get-tuple-element.2) | data formatting | bytes 393216
  33.5 0.6 %copy.20 = f32[16,512]{1,0:T(8,128)} copy(f32[16,512]{1,0:T(8,128)S(1)} %get-tuple-element.3) | data formatting | bytes 65536

commit v3 on v2

--- a/solution.py
+++ b/solution.py
@@ -102,8 +102,11 @@
     raise_faces = split_columns(raise_all)
     lower_faces = split_columns(lower_all)
     project_all = np.asarray(kron3(down, down, down), np.float32).astype(np.float64)
-    project_x = np.concatenate([project_all[:, :64], project_all[:, 448:]], axis=1)
-    late_fine = split_columns(np.concatenate([raise_all @ project_x, project_x], axis=0))
+    fine_selectors = face_selectors(P7)
+    project_late = np.concatenate(
+        [project_all @ fine_selectors[side].T for side in (0, 1, 4, 5)], axis=1
+    )
+    late_fine = split_columns(np.concatenate([raise_all @ project_late, project_late], axis=0))
     lower_x = lower_all[:, :128]
     late_coarse = split_columns(np.concatenate([raise_all @ lower_x, lower_x], axis=0))
     coarse = to_bf16(
@@ -141,6 +144,10 @@
     for where in face_slices(side):
         ref[where, :] += value[start : start + where.size]
         start += where.size
+
+
+def edge_slice(x_end, z_end):
+    return pl.ds(448 * x_end + 7 * z_end, P7, stride=8)
 
 
 def kernel(
@@ -198,6 +205,12 @@
     move_recv,
     early_send,
     early_recv,
+    wide_send,
+    wide_recv,
+    far_trace,
+    next_near,
+    corner_send,
+    corner_recv,
     extra_recv,
     move_coef,
     turned,
@@ -213,6 +226,10 @@
     early_rsem,
     extra_ssem,
     extra_rsem,
+    wide_ssem,
+    wide_rsem,
+    corner_ssem,
+    corner_rsem,
 ):
     slab, pos = lax.axis_index("slab"), lax.axis_index("curve")
     left, right = lax.rem(pos + pieces - 1, pieces), lax.rem(pos + 1, pieces)
@@ -220,8 +237,9 @@
     partner = {0: (slab, left), 1: (slab, right), 4: (below, pos), 5: (above, pos)}
 
     barrier = pltpu.get_barrier_semaphore()
-    for side in (0, 1, 4, 5):
-        pl.semaphore_signal(barrier, inc=1, device_id=partner[side], device_id_type=MESH)
+    corners = [(below, left), (below, right), (above, left), (above, right)]
+    for device in list(partner.values()) + corners:
+        pl.semaphore_signal(barrier, inc=1, device_id=device, device_id_type=MESH)
 
     pairs = [
         (state_h, state_v),
@@ -316,10 +334,193 @@
         return face_get(ref, side).astype(BF16)
 
     traces = [fine_trace(u0, side) for side in range(6)]
-    pl.semaphore_wait(barrier, 4)
+    gather_local(traces)
+
+    loads[1].wait()
+    loads[3].wait()
+    loads[9].wait()
+    for dim in range(3):
+        spread_vel = lax.dot_general(
+            vel_v[dim],
+            spread.astype(BF16),
+            (((0,), (0,)), ((), ())),
+            preferred_element_type=F32,
+        ).astype(BF16)
+        vel_rep[dim * 64 : dim * 64 + 64] = spread_vel.astype(F32)
+        speed[dim] = dot(lift_v[...], spread_vel).astype(BF16).astype(F32)
+        mortar = dot(raise_v[dim * 128 : dim * 128 + 128, :128], jnp.concatenate([spread_vel, spread_vel], axis=0))
+        vmin[dim * 128 : dim * 128 + 64] = jnp.minimum(-mortar[:64], 0.0)
+        vmin[dim * 128 + 64 : dim * 128 + 128] = jnp.minimum(mortar[64:], 0.0)
+        for end in range(2):
+            side = 2 * dim + end
+            normal = face_get(speed.at[dim], side)
+            lift_coef = STEP * (P7 * (P7 - 1) / 2.0)
+            coef[side] = lift_coef * jnp.minimum(normal if end else -normal, 0.0)
+
+    loads[4].wait()
+    loads[5].wait()
+    pre_row = jnp.zeros((1, LANES), F32)
+    stoich_row = jnp.zeros((1, LANES), F32)
+    for elem in range(ELEMS):
+        pre_row = jnp.where(lane_elem == elem, pre_s[elem], pre_row)
+    for field in range(FIELDS):
+        stoich_row = jnp.where(lane_field == field, stoich_s[field], stoich_row)
+
+    def source(u):
+        rate = (
+            pre_row
+            * jnp.exp(-ACTIVATION * jnp.exp(-u))
+            * pltpu.roll(u, LANES - 1, 1)
+            * pltpu.roll(u, LANES - 2, 1)
+        )
+        high = rate.astype(BF16)
+        low = (rate - high.astype(F32)).astype(BF16)
+        return stoich_row * dot(jnp.concatenate([high, low], axis=1), rep2)
+
+    for number in range(8, 15):
+        if number != 9:
+            loads[number].wait()
+
+    def fine_start(ref, start, out, traces):
+        scale = 1.0 if start is None else 0.5
+        along_i = []
+        for half in range(2):
+            parts = []
+            for i in range(P7):
+                at = pl.ds(i * 64 + half * 32, 32)
+                parts.append((speed[0, at, :] * ref[at, :]).astype(BF16))
+            along_i.append(dot(fine_v[:256, :], jnp.concatenate(parts, axis=0)))
+        for block in range(4):
+            at = pl.ds(block * 128, 128)
+            u = ref[at, :]
+            flux = jnp.concatenate(
+                [(speed[1, at, :] * u).astype(BF16), (speed[2, at, :] * u).astype(BF16)], axis=0
+            )
+            div = dot(fine_v[256:, :], flux) + jnp.concatenate(
+                [
+                    along_i[half][i * 32 : i * 32 + 32]
+                    for i in (2 * block, 2 * block + 1)
+                    for half in range(2)
+                ],
+                axis=0,
+            )
+            rate = STEP * (source(u) - div)
+            out[at, :] = u + rate if start is None else 0.5 * (start[at, :] + u + rate)
+        for side in range(6):
+            jump = traces[side].astype(F32)
+            if side < 4:
+                jump = jump - local_nb[side]
+            face_add(out, side, scale * (coef[side] * jump))
+
+    def late_term(number, side, scale):
+        slot = side if side < 2 else side - 2
+        arrivals[number, side].wait_recv()
+        return scale * (coef[side] * recv[number, slot].astype(F32))
+
+    def fine_end_z(number, scale, out):
+        for side in (4, 5):
+            face_add(out, side, -late_term(number, side, scale))
+
+    def fine_end_x(number, scale, out):
+        terms = [late_term(number, side, scale) for side in (0, 1)]
+        for side in (0, 1):
+            face_add(out, side, -terms[side])
+        return jnp.concatenate(terms, axis=0)
+
+    def coarse_start(c, start):
+        flux = jnp.concatenate(
+            [(vel_rep[dim * 64 : dim * 64 + 64] * c).astype(BF16) for dim in range(3)], axis=0
+        )
+        rate = STEP * (source(c) - dot(coarse_v[...], flux))
+        return c + rate if start is None else 0.5 * (start + c + rate)
+
+    def coarse_end_z(number, own, scale, partial):
+        jumps = []
+        for side in range(6):
+            near = local_nb[side] if side < 4 else recv[number, side - 2].astype(F32)
+            mine = own[side * 64 : side * 64 + 64].astype(F32)
+            jumps.append(vmin[side * 64 : side * 64 + 64] * (mine - near))
+        return partial + scale * dot(lower_v[...], split_rows(jnp.concatenate(jumps, axis=0)))
+
+    def coarse_jump_x(number):
+        return split_rows(
+            jnp.concatenate(
+                [vmin[side * 64 : side * 64 + 64] * recv[number, side].astype(F32) for side in (0, 1)],
+                axis=0,
+            )
+        )
+
+    def launch_mixed(number, fine, raised_base, table, late):
+        own, traces = [None] * 6, [None] * 6
+        for sides in ((0, 1), (4, 5), (2, 3)):
+            at = slice(sides[0] * 64, sides[0] * 64 + 128)
+            raised = raised_base[at] - dot(table[at, :], late)
+            for place, side in enumerate(sides):
+                own[side] = raised[place * 64 : place * 64 + 64]
+                traces[side] = fine_trace(fine, side)
+                mixed = jnp.where(is_switched, own[side], traces[side].astype(F32)).astype(BF16)
+                if side in (2, 3):
+                    mixes[side] = mixed
+                else:
+                    launch(number, side, mixed)
+                    mixes[side] = mixed
+        return traces, jnp.concatenate(own, axis=0).astype(BF16)
+
+    mixes = [None] * 6
+
+    fine_start(u0, None, u1, traces)
     for side in (0, 1, 4, 5):
-        launch(0, side, traces[side])
-    gather_local(traces)
+        slot, dim, end = side if side < 2 else side - 2, side // 2, side % 2
+        edges = [(end, 0), (end, 1)] if dim == 0 else [(0, end), (1, end)]
+        first = face_get(u1, side)
+        high = first.astype(BF16)
+        packed = [
+            traces[side],
+            face_get(speed.at[dim], side).astype(BF16),
+            jnp.concatenate([speed[2 - dim, edge_slice(*edge), :] for edge in edges], axis=0).astype(BF16),
+            high,
+            (first - high.astype(F32)).astype(BF16),
+        ]
+        placed = dot(jnp.concatenate(packed, axis=0), perm_far[slot])
+        wide_send[slot] = placed.astype(BF16)
+        far_trace[slot] = placed[:64]
+    for number, corner in enumerate(corners):
+        z_end, x_end = number // 2, number % 2
+        corner_send[number] = jnp.concatenate(
+            [
+                far_trace[x_end, pl.ds(7 * z_end, P7, stride=8), :],
+                far_trace[2 + z_end, pl.ds(56 * x_end, P7), :],
+            ],
+            axis=0,
+        ).astype(BF16)
+    pl.semaphore_wait(barrier, 8)
+    for number, corner in enumerate(corners):
+        copy = pltpu.make_async_remote_copy(
+            src_ref=corner_send.at[number],
+            dst_ref=corner_recv.at[3 - number],
+            send_sem=corner_ssem.at[number],
+            recv_sem=corner_rsem.at[3 - number],
+            device_id=corner,
+            device_id_type=MESH,
+        )
+        copy.start()
+        started.append(copy)
+        arrivals["corner", 3 - number] = copy
+    for part, (start_row, count) in enumerate(((0, 144), (144, 128))):
+        for side in (0, 1, 4, 5):
+            slot = side if side < 2 else side - 2
+            at = pl.ds(start_row, count)
+            copy = pltpu.make_async_remote_copy(
+                src_ref=wide_send.at[slot, at],
+                dst_ref=wide_recv.at[slot ^ 1, at],
+                send_sem=wide_ssem.at[part, slot],
+                recv_sem=wide_rsem.at[part, slot ^ 1],
+                device_id=partner[side],
+                device_id_type=MESH,
+            )
+            copy.start()
+            started.append(copy)
+            arrivals["wide", part, side ^ 1] = copy
 
     loads[6].wait()
     loads[7].wait()
@@ -363,27 +564,6 @@
         count_arrivals.append(copy)
     is_switched = switch_row > 0.5
 
-    loads[1].wait()
-    loads[3].wait()
-    loads[9].wait()
-    for dim in range(3):
-        spread_vel = lax.dot_general(
-            vel_v[dim],
-            spread.astype(BF16),
-            (((0,), (0,)), ((), ())),
-            preferred_element_type=F32,
-        ).astype(BF16)
-        vel_rep[dim * 64 : dim * 64 + 64] = spread_vel.astype(F32)
-        speed[dim] = dot(lift_v[...], spread_vel).astype(BF16).astype(F32)
-        mortar = dot(raise_v[dim * 128 : dim * 128 + 128, :128], jnp.concatenate([spread_vel, spread_vel], axis=0))
-        vmin[dim * 128 : dim * 128 + 64] = jnp.minimum(-mortar[:64], 0.0)
-        vmin[dim * 128 + 64 : dim * 128 + 128] = jnp.minimum(mortar[64:], 0.0)
-        for end in range(2):
-            side = 2 * dim + end
-            normal = face_get(speed.at[dim], side)
-            lift_coef = STEP * (P7 * (P7 - 1) / 2.0)
-            coef[side] = lift_coef * jnp.minimum(normal if end else -normal, 0.0)
-
     for side, picks, count in ((0, left_pick, left_count), (1, right_pick, right_count)):
         chosen = jnp.zeros((LANES, LANES), F32)
         for slot in range(2):
@@ -408,132 +588,51 @@
         started.append(copy)
         count_arrivals.append(copy)
 
-    loads[4].wait()
-    loads[5].wait()
-    pre_row = jnp.zeros((1, LANES), F32)
-    stoich_row = jnp.zeros((1, LANES), F32)
-    for elem in range(ELEMS):
-        pre_row = jnp.where(lane_elem == elem, pre_s[elem], pre_row)
-    for field in range(FIELDS):
-        stoich_row = jnp.where(lane_field == field, stoich_s[field], stoich_row)
-
-    def source(u):
-        rate = (
-            pre_row
-            * jnp.exp(-ACTIVATION * jnp.exp(-u))
-            * pltpu.roll(u, LANES - 1, 1)
-            * pltpu.roll(u, LANES - 2, 1)
-        )
-        high = rate.astype(BF16)
-        low = (rate - high.astype(F32)).astype(BF16)
-        return stoich_row * dot(jnp.concatenate([high, low], axis=1), rep2)
-
-    for number in range(8, 15):
-        if number != 9:
-            loads[number].wait()
-
-    def fine_start(ref, start, out, traces):
-        scale = 1.0 if start is None else 0.5
-        along_i = []
-        for half in range(2):
-            parts = []
-            for i in range(P7):
-                at = pl.ds(i * 64 + half * 32, 32)
-                parts.append((speed[0, at, :] * ref[at, :]).astype(BF16))
-            along_i.append(dot(fine_v[:256, :], jnp.concatenate(parts, axis=0)))
-        for block in range(4):
-            at = pl.ds(block * 128, 128)
-            u = ref[at, :]
-            flux = jnp.concatenate(
-                [(speed[1, at, :] * u).astype(BF16), (speed[2, at, :] * u).astype(BF16)], axis=0
-            )
-            div = dot(fine_v[256:, :], flux) + jnp.concatenate(
-                [
-                    along_i[half][i * 32 : i * 32 + 32]
-                    for i in (2 * block, 2 * block + 1)
-                    for half in range(2)
-                ],
-                axis=0,
-            )
-            rate = STEP * (source(u) - div)
-            out[at, :] = u + rate if start is None else 0.5 * (start[at, :] + u + rate)
-        for side in range(6):
-            jump = traces[side].astype(F32)
-            if side < 4:
-                jump = jump - local_nb[side]
-            face_add(out, side, scale * (coef[side] * jump))
-
-    def late_term(number, side, scale):
+    for side in (4, 5, 0, 1):
         slot = side if side < 2 else side - 2
-        arrivals[number, side].wait_recv()
-        return scale * (coef[side] * recv[number, slot].astype(F32))
-
-    def fine_end_z(number, scale, out):
-        for side in (4, 5):
-            face_add(out, side, -late_term(number, side, scale))
-
-    def fine_end_x(number, scale, out):
-        terms = [late_term(number, side, scale) for side in (0, 1)]
-        for side in (0, 1):
-            face_add(out, side, -terms[side])
-        return jnp.concatenate(terms, axis=0)
-
-    def coarse_start(c, start):
-        flux = jnp.concatenate(
-            [(vel_rep[dim * 64 : dim * 64 + 64] * c).astype(BF16) for dim in range(3)], axis=0
-        )
-        rate = STEP * (source(c) - dot(coarse_v[...], flux))
-        return c + rate if start is None else 0.5 * (start + c + rate)
-
-    def coarse_end_z(number, own, scale, partial):
-        jumps = []
-        for side in range(6):
-            near = local_nb[side] if side < 4 else recv[number, side - 2].astype(F32)
-            mine = own[side * 64 : side * 64 + 64].astype(F32)
-            jumps.append(vmin[side * 64 : side * 64 + 64] * (mine - near))
-        return partial + scale * dot(lower_v[...], split_rows(jnp.concatenate(jumps, axis=0)))
-
-    def coarse_jump_x(number):
-        return split_rows(
-            jnp.concatenate(
-                [vmin[side * 64 : side * 64 + 64] * recv[number, side].astype(F32) for side in (0, 1)],
-                axis=0,
-            )
-        )
-
-    def launch_mixed(number, fine, raised_base, table, late):
-        own, traces = [None] * 6, [None] * 6
-        for sides in ((0, 1), (4, 5), (2, 3)):
-            at = slice(sides[0] * 64, sides[0] * 64 + 128)
-            raised = raised_base[at] - dot(table[at, :], late)
-            for place, side in enumerate(sides):
-                own[side] = raised[place * 64 : place * 64 + 64]
-                traces[side] = fine_trace(fine, side)
-                mixed = jnp.where(is_switched, own[side], traces[side].astype(F32)).astype(BF16)
-                if side in (2, 3):
-                    mixes[side] = mixed
-                else:
-                    launch(number, side, mixed)
-                    mixes[side] = mixed
-        return traces, jnp.concatenate(own, axis=0).astype(BF16)
-
-    mixes = [None] * 6
-
-    fine_start(u0, None, u1, traces)
-    fine_end_z(0, 1.0, u1)
-    fine_end_x(0, 1.0, u1)
-    traces = [None] * 6
-    for side in (0, 1, 4, 5):
-        traces[side] = fine_trace(u1, side)
-        launch(1, side, traces[side])
-    for side in (2, 3):
-        traces[side] = fine_trace(u1, side)
-    gather_local(traces)
-    fine_start(u1, u0, u2, traces)
-    fine_end_z(1, 0.5, u2)
+        arrivals["wide", 0, side].wait_recv()
+        face_add(u1, side, -(coef[side] * wide_recv[slot, pl.ds(0, 64), :].astype(F32)))
+    next_traces = [fine_trace(u1, side) for side in range(6)]
+    gather_local(next_traces)
+    fine_start(u1, u0, u2, next_traces)
     c0 = dot(project_v[...], split_rows(u2[...]))
     raised = dot(raise_v[...], split_rows(c0))
-    late = split_rows(fine_end_x(1, 0.5, u2))
+
+    lift_coef = STEP * (P7 * (P7 - 1) / 2.0)
+    for number in range(4):
+        arrivals["corner", number].wait_recv()
+    corner_values = [corner_recv[number].astype(F32) for number in range(4)]
+    late = []
+    for side in (0, 1, 4, 5):
+        slot, dim, end = side if side < 2 else side - 2, side // 2, side % 2
+        arrivals["wide", 1, side].wait_recv()
+        got = wide_recv[slot].astype(F32)
+        normal = -got[64:128] if end else got[64:128]
+        first = got[144:208] + got[208:272]
+        first = first - lift_coef * jnp.minimum(normal, 0.0) * traces[side].astype(F32)
+        if dim == 0:
+            around = [corner_values[end][8:16], corner_values[2 + end][8:16]]
+        else:
+            around = [corner_values[2 * end][0:8], corner_values[2 * end + 1][0:8]]
+        around = lax.dot_general(
+            jnp.concatenate(around, axis=0).astype(BF16),
+            perm_far[slot],
+            (((1,), (1,)), ((), ())),
+            preferred_element_type=F32,
+        )
+        low_edge = lift_coef * jnp.minimum(-got[128:136], 0.0) * around[:8]
+        high_edge = lift_coef * jnp.minimum(got[136:144], 0.0) * around[8:]
+        next_near[slot] = first
+        if dim == 0:
+            next_near[slot, pl.ds(0, P7, stride=8), :] -= low_edge
+            next_near[slot, pl.ds(7, P7, stride=8), :] -= high_edge
+        else:
+            next_near[slot, pl.ds(0, P7), :] -= low_edge
+            next_near[slot, pl.ds(56, P7), :] -= high_edge
+        late.append(0.5 * (coef[side] * next_near[slot].astype(BF16).astype(F32)))
+    for place, side in enumerate((0, 1, 4, 5)):
+        face_add(u2, side, -late[place])
+    late = split_rows(jnp.concatenate(late, axis=0))
 
     traces, own = launch_mixed(2, u2, raised, late_fine_v, late)
     gather_local(mixes)
@@ -709,6 +808,12 @@
                 vm((2, 2, FIELDS, 512), F32),
                 vm((2, 3 * LANES, LANES), BF16),
                 vm((2, 3 * LANES, LANES), BF16),
+                vm((4, 272, LANES), BF16),
+                vm((4, 272, LANES), BF16),
+                vm((4, 64, LANES), F32),
+                vm((4, 64, LANES), F32),
+                vm((4, 16, LANES), BF16),
+                vm((4, 16, LANES), BF16),
                 vm((2, 3, 64, LANES), BF16),
                 vm((4, 64, LANES), F32),
                 vm((LANES, LANES), F32),
@@ -724,6 +829,10 @@
                 dma((2,)),
                 dma((2, 3)),
                 dma((2, 3)),
+                dma((2, 4)),
+                dma((2, 4)),
+                dma((4,)),
+                dma((4,)),
             ],
             compiler_params=pltpu.CompilerParams(
                 collective_id=0, has_side_effects=True, vmem_limit_bytes=62 * 2**20

time: 34.3 us -> 33.2 us (0.968)
  Pallas kernels: 32.2 us -> 31.1 us
    pallas_call x1, Pallas kernels: 32.2 us -> 31.1 us  [per_device(): pl.pallas_call(functools.partial(kernel, slabs, pieces), out_shape=(pltpu...]
where the time goes in v3:
time: 33.2 us; the launch traced here: 33 us
  Pallas kernels  31.1 us (94%)
  local copies, waits for them, and re-layouts  1.29 us (4%)
  between operations  0.64 us (2%)
    pallas_call x1, Pallas kernels, per_device(): pl.pallas_call(functools.partial(kernel, slabs, pieces), out_shape=(pltpu...  31.1 us
    unnamed x2, local copies, waits for them, and re-layouts  1.29 us

profile of v3, /device:TPU:1, one launch (start us, length us, event | category | flops | bytes accessed | tf_op | source)
XLA Modules:
  0.0 33.0 jit_solution(11781837725194805190)
XLA Ops:
  0.6 31.1 %shard_map.158 = (f32[12,8,512]{2,1,0:T(8,128)S(1)}, f32[16,512]{1,0:T(8,128)S(1)}) custom-call(f32[16,8,512]{2,1,0:T(8,128)} %state_h.1, bf16[3,16,64]{2,1,0:T(8,128)(2,1)} %bitcast.2, s32[6,16]{1,0:T(8,128)} %bitcast.3, f32[16]{0:T(128)} %pre_h.1, f32[8]{0:T(128)} %stoich_h.1, s32[16]{0:T(128)} %switch_h.1, s32[16]{0:T(128)} %owner_h.1, ...), custom_call_target="tpu_custom_call" | custom-call | tf_op jit(solution)/shard_map/pallas_call | solution.py:772
  31.8 0.7 %copy.19 = f32[12,8,512]{2,1,0:T(8,128)} copy(f32[12,8,512]{2,1,0:T(8,128)S(1)} %get-tuple-element.2) | data formatting | bytes 393216
  32.4 0.6 %copy.20 = f32[16,512]{1,0:T(8,128)} copy(f32[16,512]{1,0:T(8,128)S(1)} %get-tuple-element.3) | data formatting | bytes 65536

commit v4 on v3

--- a/solution.py
+++ b/solution.py
@@ -262,8 +262,8 @@
         pltpu.make_async_copy(source, target, load_sem.at[number])
         for number, (source, target) in enumerate(pairs)
     ]
-    for load in loads:
-        load.start()
+    for number in (0, 2, 1, 3, 8, 4, 5, 6, 7):
+        loads[number].start()
 
     lane_row = lax.broadcasted_iota(jnp.int32, (1, LANES), 1)
     lane_elem = lane_row // FIELDS
@@ -278,6 +278,8 @@
     rep2 = jnp.concatenate([rep, rep], axis=0)
 
     loads[0].wait()
+    for load in loads[9:]:
+        load.start()
     u0[...] = jnp.transpose(state_v[...].reshape(LANES, 512))
 
     loads[2].wait()
@@ -338,7 +340,6 @@
 
     loads[1].wait()
     loads[3].wait()
-    loads[9].wait()
     for dim in range(3):
         spread_vel = lax.dot_general(
             vel_v[dim],
@@ -348,9 +349,6 @@
         ).astype(BF16)
         vel_rep[dim * 64 : dim * 64 + 64] = spread_vel.astype(F32)
         speed[dim] = dot(lift_v[...], spread_vel).astype(BF16).astype(F32)
-        mortar = dot(raise_v[dim * 128 : dim * 128 + 128, :128], jnp.concatenate([spread_vel, spread_vel], axis=0))
-        vmin[dim * 128 : dim * 128 + 64] = jnp.minimum(-mortar[:64], 0.0)
-        vmin[dim * 128 + 64 : dim * 128 + 128] = jnp.minimum(mortar[64:], 0.0)
         for end in range(2):
             side = 2 * dim + end
             normal = face_get(speed.at[dim], side)
@@ -377,9 +375,7 @@
         low = (rate - high.astype(F32)).astype(BF16)
         return stoich_row * dot(jnp.concatenate([high, low], axis=1), rep2)
 
-    for number in range(8, 15):
-        if number != 9:
-            loads[number].wait()
+    loads[8].wait()
 
     def fine_start(ref, start, out, traces):
         scale = 1.0 if start is None else 0.5
@@ -588,6 +584,17 @@
         started.append(copy)
         count_arrivals.append(copy)
 
+    for load in loads[9:]:
+        load.wait()
+    for dim in range(3):
+        spread_vel = vel_rep[dim * 64 : dim * 64 + 64].astype(BF16)
+        mortar = dot(
+            raise_v[dim * 128 : dim * 128 + 128, :128],
+            jnp.concatenate([spread_vel, spread_vel], axis=0),
+        )
+        vmin[dim * 128 : dim * 128 + 64] = jnp.minimum(-mortar[:64], 0.0)
+        vmin[dim * 128 + 64 : dim * 128 + 128] = jnp.minimum(mortar[64:], 0.0)
+
     for side in (4, 5, 0, 1):
         slot = side if side < 2 else side - 2
         arrivals["wide", 0, side].wait_recv()
@@ -599,17 +606,28 @@
     raised = dot(raise_v[...], split_rows(c0))
 
     lift_coef = STEP * (P7 * (P7 - 1) / 2.0)
+    edge_coef = {}
+    for side in (0, 1, 4, 5):
+        slot, end = side if side < 2 else side - 2, side % 2
+        normal = wide_recv[slot, pl.ds(64, 64), :].astype(F32)
+        normal = -normal if end else normal
+        next_near[slot] = lift_coef * jnp.minimum(normal, 0.0) * traces[side].astype(F32)
+        edge = wide_recv[slot, pl.ds(128, 16), :].astype(F32)
+        edge_coef[side] = [
+            lift_coef * jnp.minimum(-edge[:8], 0.0),
+            lift_coef * jnp.minimum(edge[8:], 0.0),
+        ]
+    for side in (4, 5, 0, 1):
+        slot = side if side < 2 else side - 2
+        arrivals["wide", 1, side].wait_recv()
+        got = wide_recv[slot, pl.ds(144, 128), :].astype(F32)
+        next_near[slot] = got[:64] + got[64:] - next_near[slot]
     for number in range(4):
         arrivals["corner", number].wait_recv()
     corner_values = [corner_recv[number].astype(F32) for number in range(4)]
     late = []
     for side in (0, 1, 4, 5):
         slot, dim, end = side if side < 2 else side - 2, side // 2, side % 2
-        arrivals["wide", 1, side].wait_recv()
-        got = wide_recv[slot].astype(F32)
-        normal = -got[64:128] if end else got[64:128]
-        first = got[144:208] + got[208:272]
-        first = first - lift_coef * jnp.minimum(normal, 0.0) * traces[side].astype(F32)
         if dim == 0:
             around = [corner_values[end][8:16], corner_values[2 + end][8:16]]
         else:
@@ -620,15 +638,10 @@
             (((1,), (1,)), ((), ())),
             preferred_element_type=F32,
         )
-        low_edge = lift_coef * jnp.minimum(-got[128:136], 0.0) * around[:8]
-        high_edge = lift_coef * jnp.minimum(got[136:144], 0.0) * around[8:]
-        next_near[slot] = first
-        if dim == 0:
-            next_near[slot, pl.ds(0, P7, stride=8), :] -= low_edge
-            next_near[slot, pl.ds(7, P7, stride=8), :] -= high_edge
-        else:
-            next_near[slot, pl.ds(0, P7), :] -= low_edge
-            next_near[slot, pl.ds(56, P7), :] -= high_edge
+        for which in range(2):
+            term = edge_coef[side][which] * around[8 * which : 8 * which + 8]
+            at = pl.ds(7 * which, P7, stride=8) if dim == 0 else pl.ds(56 * which, P7)
+            next_near[slot, at, :] -= term
         late.append(0.5 * (coef[side] * next_near[slot].astype(BF16).astype(F32)))
     for place, side in enumerate((0, 1, 4, 5)):
         face_add(u2, side, -late[place])
@@ -757,6 +770,17 @@
         copy.wait_send()
 
 
+def store_kernel(held7, held3, out7, out3, sem):
+    copies = [
+        pltpu.make_async_copy(held7, out7, sem.at[0]),
+        pltpu.make_async_copy(held3, out3, sem.at[1]),
+    ]
+    for copy in copies:
+        copy.start()
+    for copy in copies:
+        copy.wait()
+
+
 def solution(mesh):
     slabs, pieces = mesh.shape["slab"], mesh.shape["curve"]
     tables = make_tables()
@@ -769,7 +793,7 @@
         )
         vm, sm, dma = pltpu.VMEM, pltpu.SMEM, pltpu.SemaphoreType.DMA
         nodes = (512, LANES)
-        return pl.pallas_call(
+        held = pl.pallas_call(
             functools.partial(kernel, slabs, pieces),
             out_shape=(
                 pltpu.VMEM((HOLD7, FIELDS, 512), F32),
@@ -838,6 +862,17 @@
                 collective_id=0, has_side_effects=True, vmem_limit_bytes=62 * 2**20
             ),
         )(*operands)
+        return pl.pallas_call(
+            store_kernel,
+            out_shape=(
+                jax.ShapeDtypeStruct((HOLD7, FIELDS, 512), F32),
+                jax.ShapeDtypeStruct((ELEMS, 512), F32),
+            ),
+            in_specs=[pl.BlockSpec(memory_space=pl.ANY)] * 2,
+            out_specs=[pl.BlockSpec(memory_space=pltpu.HBM)] * 2,
+            scratch_shapes=[dma((2,))],
+            compiler_params=pltpu.CompilerParams(vmem_limit_bytes=2**20),
+        )(*held)
 
     return jax.shard_map(
         per_device,

time: 33.2 us -> 32.2 us (0.970)
  local copies, waits for them, and re-layouts: 1.29 us -> 0 us
    unnamed x2 -> x0, local copies, waits for them, and re-layouts: 1.29 us -> none
    pallas_call x0 -> x1, Pallas kernels: none -> 0.7 us  [per_device(): pl.pallas_call(store_kernel, out_shape=(jax.ShapeDtypeStruct((HOLD7, FIEL...]
    pallas_call x1, Pallas kernels: 31.1 us -> 30.7 us  [per_device(): pl.pallas_call(functools.partial(kernel, slabs, pieces), out_shape=(pltpu...]
where the time goes in v4:
time: 32.2 us; the launch traced here: 32 us
  Pallas kernels  31.4 us (98%)
  between operations  0.64 us (2%)
    pallas_call x1, Pallas kernels, per_device(): pl.pallas_call(functools.partial(kernel, slabs, pieces), out_shape=(pltpu...  30.7 us
    pallas_call x1, Pallas kernels, per_device(): pl.pallas_call(store_kernel, out_shape=(jax.ShapeDtypeStruct((HOLD7, FIEL...  0.7 us

profile of v4, /device:TPU:1, one launch (start us, length us, event | category | flops | bytes accessed | tf_op | source)
XLA Modules:
  0.0 32.0 jit_solution(5717943580289930771)
XLA Ops:
  0.6 30.7 %shard_map.158 = (f32[12,8,512]{2,1,0:T(8,128)S(1)}, f32[16,512]{1,0:T(8,128)S(1)}) custom-call(f32[16,8,512]{2,1,0:T(8,128)} %state_h.1, bf16[3,16,64]{2,1,0:T(8,128)(2,1)} %bitcast.2, s32[6,16]{1,0:T(8,128)} %bitcast.3, f32[16]{0:T(128)} %pre_h.1, f32[8]{0:T(128)} %stoich_h.1, s32[16]{0:T(128)} %switch_h.1, s32[16]{0:T(128)} %owner_h.1, ...), custom_call_target="tpu_custom_call" | custom-call | tf_op jit(solution)/shard_map/pallas_call | solution.py:796
  31.3 0.7 %shard_map.159 = (f32[12,8,512]{2,1,0:T(8,128)}, f32[16,512]{1,0:T(8,128)}) custom-call(f32[12,8,512]{2,1,0:T(8,128)S(1)} %get-tuple-element.4.held7, f32[16,512]{1,0:T(8,128)S(1)} %get-tuple-element.5.held3), custom_call_target="tpu_custom_call" | custom-call | tf_op jit(solution)/shard_map/pallas_call | solution.py:865

commit v5 on v4

--- a/solution.py
+++ b/solution.py
@@ -106,13 +106,13 @@
     project_late = np.concatenate(
         [project_all @ fine_selectors[side].T for side in (0, 1, 4, 5)], axis=1
     )
-    late_fine = split_columns(np.concatenate([raise_all @ project_late, project_late], axis=0))
-    lower_x = lower_all[:, :128]
-    late_coarse = split_columns(np.concatenate([raise_all @ lower_x, lower_x], axis=0))
+    lower_late = np.concatenate([lower_all[:, :128], lower_all[:, 256:]], axis=1)
+    late_raise = to_bf16(np.concatenate([raise_all @ project_late, raise_all @ lower_late], axis=0))
+    late_nodes = split_columns(np.concatenate([project_late, lower_late], axis=0))
     coarse = to_bf16(
         np.concatenate([kron3(d3, i3, i3), kron3(i3, d3, i3), kron3(i3, i3, d3)], axis=1)
     )
-    return fine, lift, project, raise_faces, lower_faces, coarse, late_fine, late_coarse
+    return fine, lift, project, raise_faces, lower_faces, coarse, late_raise, late_nodes
 
 
 def dot(a, b):
@@ -166,8 +166,8 @@
     raise_h,
     lower_h,
     coarse_h,
-    late_fine_h,
-    late_coarse_h,
+    late_raise_h,
+    late_nodes_h,
     out7_v,
     out3_v,
     state_v,
@@ -183,8 +183,8 @@
     raise_v,
     lower_v,
     coarse_v,
-    late_fine_v,
-    late_coarse_v,
+    late_raise_v,
+    late_nodes_v,
     u0,
     u1,
     u2,
@@ -238,7 +238,7 @@
 
     barrier = pltpu.get_barrier_semaphore()
     corners = [(below, left), (below, right), (above, left), (above, right)]
-    for device in list(partner.values()) + corners:
+    for device in corners + list(partner.values()):
         pl.semaphore_signal(barrier, inc=1, device_id=device, device_id_type=MESH)
 
     pairs = [
@@ -255,8 +255,8 @@
         (project_h, project_v),
         (lower_h, lower_v),
         (coarse_h, coarse_v),
-        (late_fine_h, late_fine_v),
-        (late_coarse_h, late_coarse_v),
+        (late_raise_h, late_raise_v),
+        (late_nodes_h, late_nodes_v),
     ]
     loads = [
         pltpu.make_async_copy(source, target, load_sem.at[number])
@@ -418,10 +418,8 @@
             face_add(out, side, -late_term(number, side, scale))
 
     def fine_end_x(number, scale, out):
-        terms = [late_term(number, side, scale) for side in (0, 1)]
         for side in (0, 1):
-            face_add(out, side, -terms[side])
-        return jnp.concatenate(terms, axis=0)
+            face_add(out, side, -late_term(number, side, scale))
 
     def coarse_start(c, start):
         flux = jnp.concatenate(
@@ -430,27 +428,29 @@
         rate = STEP * (source(c) - dot(coarse_v[...], flux))
         return c + rate if start is None else 0.5 * (start + c + rate)
 
-    def coarse_end_z(number, own, scale, partial):
+    def coarse_local(own, scale, partial):
         jumps = []
         for side in range(6):
-            near = local_nb[side] if side < 4 else recv[number, side - 2].astype(F32)
-            mine = own[side * 64 : side * 64 + 64].astype(F32)
-            jumps.append(vmin[side * 64 : side * 64 + 64] * (mine - near))
+            jump = own[side * 64 : side * 64 + 64].astype(F32)
+            if side < 4:
+                jump = jump - local_nb[side]
+            jumps.append(vmin[side * 64 : side * 64 + 64] * jump)
         return partial + scale * dot(lower_v[...], split_rows(jnp.concatenate(jumps, axis=0)))
 
-    def coarse_jump_x(number):
-        return split_rows(
-            jnp.concatenate(
-                [vmin[side * 64 : side * 64 + 64] * recv[number, side].astype(F32) for side in (0, 1)],
-                axis=0,
+    def coarse_late(number):
+        terms = []
+        for slot, side in enumerate((0, 1, 4, 5)):
+            terms.append(vmin[side * 64 : side * 64 + 64] * recv[number, slot].astype(F32))
+        return jnp.concatenate(terms, axis=0)
+
+    def launch_mixed(number, fine, raised_base, first_row, late, order, after=None):
+        late = late.astype(BF16)
+        own, traces = [None] * 6, [None] * 6
+        for sides in order:
+            at = slice(sides[0] * 64, sides[0] * 64 + 128)
+            raised = raised_base[at] - dot(
+                late_raise_v[pl.ds(first_row + sides[0] * 64, 128), :], late
             )
-        )
-
-    def launch_mixed(number, fine, raised_base, table, late):
-        own, traces = [None] * 6, [None] * 6
-        for sides in ((0, 1), (4, 5), (2, 3)):
-            at = slice(sides[0] * 64, sides[0] * 64 + 128)
-            raised = raised_base[at] - dot(table[at, :], late)
             for place, side in enumerate(sides):
                 own[side] = raised[place * 64 : place * 64 + 64]
                 traces[side] = fine_trace(fine, side)
@@ -460,6 +460,8 @@
                 else:
                     launch(number, side, mixed)
                     mixes[side] = mixed
+            if after is not None:
+                after(sides)
         return traces, jnp.concatenate(own, axis=0).astype(BF16)
 
     mixes = [None] * 6
@@ -645,11 +647,13 @@
         late.append(0.5 * (coef[side] * next_near[slot].astype(BF16).astype(F32)))
     for place, side in enumerate((0, 1, 4, 5)):
         face_add(u2, side, -late[place])
-    late = split_rows(jnp.concatenate(late, axis=0))
-
-    traces, own = launch_mixed(2, u2, raised, late_fine_v, late)
+    late = jnp.concatenate(late, axis=0)
+
+    traces, own = launch_mixed(
+        2, u2, raised, 0, late, ((0, 1), (4, 5), (2, 3))
+    )
     gather_local(mixes)
-    c0 = c0 - dot(late_fine_v[384:, :], late)
+    c0 = c0 - dot(late_nodes_v[:64, :], split_rows(late))
     fine_start(u2, None, u3, traces)
     partial = coarse_start(c0, None)
     for copy in count_arrivals:
@@ -659,12 +663,11 @@
         normal = early_recv[0, at, :].astype(F32) + early_recv[1, at, :].astype(F32)
         lift_coef = 0.5 * STEP * (P7 * (P7 - 1) / 2.0)
         move_coef[place] = lift_coef * jnp.minimum(normal if side % 2 else -normal, 0.0)
+    c1 = coarse_local(own, 1.0, partial)
+    raised = dot(raise_v[...], split_rows(c1))
     fine_end_z(2, 1.0, u3)
-    c1 = coarse_end_z(2, own, 1.0, partial)
-    raised = dot(raise_v[...], split_rows(c1))
     fine_end_x(2, 1.0, u3)
-    late = coarse_jump_x(2)
-    traces, own = launch_mixed(3, u3, raised, late_coarse_v, late)
+    late = coarse_late(2)
 
     left2, right2 = lax.rem(pos + pieces - 2, pieces), lax.rem(pos + 2, pieces)
     extras = {
@@ -676,21 +679,30 @@
         (1, 0): (1, (slab, right2)),
     }
     extra_copies = []
-    for (toward, kind), (slot, device) in extras.items():
-        place = 3 - kind if kind else 0
-        copy = pltpu.make_async_remote_copy(
-            src_ref=send.at[3, slot],
-            dst_ref=extra_recv.at[1 - toward, place],
-            send_sem=extra_ssem.at[toward, kind],
-            recv_sem=extra_rsem.at[1 - toward, place],
-            device_id=device,
-            device_id_type=MESH,
-        )
-        copy.start()
-        started.append(copy)
-        extra_copies.append(copy)
+
+    def launch_extras(sides):
+        for (toward, kind), (slot, device) in extras.items():
+            if (kind == 0) != (0 in sides) or 2 in sides:
+                continue
+            place = 3 - kind if kind else 0
+            copy = pltpu.make_async_remote_copy(
+                src_ref=send.at[3, slot],
+                dst_ref=extra_recv.at[1 - toward, place],
+                send_sem=extra_ssem.at[toward, kind],
+                recv_sem=extra_rsem.at[1 - toward, place],
+                device_id=device,
+                device_id_type=MESH,
+            )
+            copy.start()
+            started.append(copy)
+            extra_copies.append(copy)
+
+    earlier = list(started)
+    started.clear()
+    traces, own = launch_mixed(
+        3, u3, raised, 384, late, ((4, 5), (0, 1), (2, 3)), launch_extras
+    )
     gather_local(mixes)
-    c1 = c1 - dot(late_coarse_v[384:, :], late)
     fine_start(u3, u2, u1, traces)
 
     def turn_home():
@@ -715,12 +727,15 @@
         copy.start()
         started.append(copy)
         extra_copies.append(copy)
+    c1 = c1 - dot(late_nodes_v[64:, :], split_rows(late))
     partial = coarse_start(c1, c0)
     u3[...] = jnp.zeros_like(u3)
+    for copy in earlier:
+        copy.wait_send()
+    c2 = coarse_local(own, 0.5, partial)
     fine_end_z(3, 0.5, u1)
-    c2 = coarse_end_z(3, own, 0.5, partial)
     fine_end_x(3, 0.5, u1)
-    c2 = c2 - 0.5 * dot(late_coarse_v[384:, :], coarse_jump_x(3))
+    c2 = c2 - 0.5 * dot(late_nodes_v[64:, :], split_rows(coarse_late(3)))
 
     c2 = jnp.where(is_switched, c2, 0.0)
     turned[...] = jnp.transpose(jnp.concatenate([c2, pltpu.roll(c2, LANES - 1, 1)], axis=0))

time: 32.2 us -> 31.6 us (0.981)
  Pallas kernels: 31.4 us -> 30.9 us
    pallas_call x1, Pallas kernels: 30.7 us -> 30.2 us  [per_device(): pl.pallas_call(functools.partial(kernel, slabs, pieces), out_shape=(pltpu...]
where the time goes in v5:
time: 31.6 us; the launch traced here: 31.5 us
  Pallas kernels  30.9 us (98%)
  between operations  0.64 us (2%)
    pallas_call x1, Pallas kernels, per_device(): pl.pallas_call(functools.partial(kernel, slabs, pieces), out_shape=(pltpu...  30.2 us
    pallas_call x1, Pallas kernels, per_device(): pl.pallas_call(store_kernel, out_shape=(jax.ShapeDtypeStruct((HOLD7, FIEL...  0.7 us

profile of v5, /device:TPU:1, one launch (start us, length us, event | category | flops | bytes accessed | tf_op | source)
XLA Modules:
  0.0 31.5 jit_solution(14367668785663742878)
XLA Ops:
  0.6 30.2 %shard_map.158 = (f32[12,8,512]{2,1,0:T(8,128)S(1)}, f32[16,512]{1,0:T(8,128)S(1)}) custom-call(f32[16,8,512]{2,1,0:T(8,128)} %state_h.1, bf16[3,16,64]{2,1,0:T(8,128)(2,1)} %bitcast.2, s32[6,16]{1,0:T(8,128)} %bitcast.3, f32[16]{0:T(128)} %pre_h.1, f32[8]{0:T(128)} %stoich_h.1, s32[16]{0:T(128)} %switch_h.1, s32[16]{0:T(128)} %owner_h.1, ...), custom_call_target="tpu_custom_call" | custom-call | tf_op jit(solution)/shard_map/pallas_call | solution.py:811
  30.8 0.7 %shard_map.159 = (f32[12,8,512]{2,1,0:T(8,128)}, f32[16,512]{1,0:T(8,128)}) custom-call(f32[12,8,512]{2,1,0:T(8,128)S(1)} %get-tuple-element.4.held7, f32[16,512]{1,0:T(8,128)S(1)} %get-tuple-element.5.held3), custom_call_target="tpu_custom_call" | custom-call | tf_op jit(solution)/shard_map/pallas_call | solution.py:880

commit v6 on v5

--- a/solution.py
+++ b/solution.py
@@ -195,6 +195,8 @@
     vmin,
     perm_far,
     perm_near,
+    origin,
+    has_origin,
     local_nb,
     send,
     recv,
@@ -311,9 +313,17 @@
         else:
             perm_far[side - 2] = far
 
+    lane_numbers = lax.broadcasted_iota(jnp.int32, (64, LANES), 1).astype(F32).astype(BF16)
+    for slot in range(4):
+        origin[slot] = dot(lane_numbers, perm_far[slot]).astype(jnp.int32)
+        has_origin[slot] = dot(jnp.ones((64, LANES), BF16), perm_far[slot])
+
     def launch(number, side, trace):
         slot = side if side < 2 else side - 2
-        send[number, slot] = dot(trace, perm_far[slot]).astype(BF16)
+        moved = jnp.take_along_axis(
+            trace.astype(F32), origin[slot], axis=1, mode="promise_in_bounds"
+        )
+        send[number, slot] = jnp.where(has_origin[slot] > 0.5, moved, 0.0).astype(BF16)
         copy = pltpu.make_async_remote_copy(
             src_ref=send.at[number, slot],
             dst_ref=recv.at[number, slot ^ 1],
@@ -837,6 +847,8 @@
                 vm((384, LANES), F32),
                 vm((4, LANES, LANES), BF16),
                 vm((4, LANES, LANES), BF16),
+                vm((4, 64, LANES), jnp.int32),
+                vm((4, 64, LANES), F32),
                 vm((4, 64, LANES), F32),
                 vm((4, 4, 64, LANES), BF16),
                 vm((4, 4, 64, LANES), BF16),

time: 31.6 us -> 31.4 us (level)
  no operation moved by 1% of the time
where the time goes in v6:
time: 31.4 us; the launch traced here: 31.2 us
  Pallas kernels  30.6 us (97%)
  between operations  0.64 us (2%)
    pallas_call x1, Pallas kernels, per_device(): pl.pallas_call(functools.partial(kernel, slabs, pieces), out_shape=(pltpu...  29.9 us
    pallas_call x1, Pallas kernels, per_device(): pl.pallas_call(store_kernel, out_shape=(jax.ShapeDtypeStruct((HOLD7, FIEL...  0.7 us

profile of v6, /device:TPU:1, one launch (start us, length us, event | category | flops | bytes accessed | tf_op | source)
XLA Modules:
  0.0 31.2 jit_solution(8828776411172453494)
XLA Ops:
  0.6 29.9 %shard_map.158 = (f32[12,8,512]{2,1,0:T(8,128)S(1)}, f32[16,512]{1,0:T(8,128)S(1)}) custom-call(f32[16,8,512]{2,1,0:T(8,128)} %state_h.1, bf16[3,16,64]{2,1,0:T(8,128)(2,1)} %bitcast.2, s32[6,16]{1,0:T(8,128)} %bitcast.3, f32[16]{0:T(128)} %pre_h.1, f32[8]{0:T(128)} %stoich_h.1, s32[16]{0:T(128)} %switch_h.1, s32[16]{0:T(128)} %owner_h.1, ...), custom_call_target="tpu_custom_call" | custom-call | tf_op jit(solution)/shard_map/pallas_call | solution.py:821
  30.5 0.7 %shard_map.159 = (f32[12,8,512]{2,1,0:T(8,128)}, f32[16,512]{1,0:T(8,128)}) custom-call(f32[12,8,512]{2,1,0:T(8,128)S(1)} %get-tuple-element.4.held7, f32[16,512]{1,0:T(8,128)S(1)} %get-tuple-element.5.held3), custom_call_target="tpu_custom_call" | custom-call | tf_op jit(solution)/shard_map/pallas_call | solution.py:892
